TPU v7x, 32 devices: a whole 2x2x4 slice. The times are simulated.
32 devices in a mesh: dp: 4 (over x, core), fsdp: 8 (over z, y).
Axes of the slice: x: 2, y: 2, z: 4, core: 2. Of those that a mesh axis runs over, the one named last changes fastest.
Arguments:
- tokens: bfloat16 [4096, 2048], P(('dp', 'fsdp')), may hold values from -6 to 6
- triple_weight: bfloat16 [2048, 6144], P(('dp', 'fsdp')), may hold values from -0.125 to 0.125
- output_weight: bfloat16 [2048, 2048], P(('dp', 'fsdp')), may hold values from -1 to 1
- up_weight: bfloat16 [2048, 8192], P(('dp', 'fsdp')), may hold values from -0.125 to 0.125
- down_weight: bfloat16 [8192, 2048], P(('dp', 'fsdp')), may hold values from -0.0625 to 0.0625
- first_gain: bfloat16 [2048], P(('dp', 'fsdp')), may hold values from 0.5 to 1.5
- second_gain: bfloat16 [2048], P(('dp', 'fsdp')), may hold values from 0.5 to 1.5
- cotangent: bfloat16 [4096, 2048], P(('dp', 'fsdp')), may hold values from -6 to 6
- frame_counts: int32 [4, 2], P('dp'), may hold values from 1 to 4
- text_counts: int32 [4, 2, 4], P('dp'), may hold values from 0 to 32
- action_counts: int32 [4, 2, 4], P('dp'), may hold values from 0 to 2
Outputs:
- layer_output: bfloat16 [4096, 2048], P(('dp', 'fsdp'))
- token_grad: bfloat16 [4096, 2048], P(('dp', 'fsdp'))
- triple_grad: float32 [2048, 6144], P(('dp', 'fsdp'))
- output_grad: float32 [2048, 2048], P(('dp', 'fsdp'))
- up_grad: float32 [2048, 8192], P(('dp', 'fsdp'))
- down_grad: float32 [8192, 2048], P(('dp', 'fsdp'))
- first_gain_grad: float32 [2048], P(('dp', 'fsdp'))
- second_gain_grad: float32 [2048], P(('dp', 'fsdp'))
All inputs are finite; a program needn't handle non-finite values.
Results may differ from a plain program's by a relative error of at most 0.015.
Values may be sent and summed in bfloat16 or wider, within the bound.
No kernel may reach another device: no remote copies, remote signals or barrier semaphores. Data moves between devices by JAX's collectives and lax.ppermute only.
A program may use at most 512 MiB of HBM per device.

v0:
```python
import math

import jax
import jax.numpy as jnp
from jax import lax
from jax.experimental import pallas as pl
from jax.experimental.pallas import tpu as pltpu
from jax.sharding import PartitionSpec as P

HEADS = 16
HEAD = 128
IMG = 576


EPSILON = 1e-05
MASKED = -1e30


def clip_layout(frame_counts, text_counts, action_counts, pack_length):
    frame_slot = jnp.arange(text_counts.shape[-1], dtype=jnp.int32)
    frame_live = frame_slot < frame_counts[..., None]
    frame_sizes = jnp.where(frame_live, IMG + text_counts + action_counts, 0)
    clip_lengths = jnp.sum(frame_sizes, axis=-1)
    first_end = clip_lengths[..., 0:1]
    second_end = first_end + clip_lengths[..., 1:2]
    places = jnp.arange(pack_length, dtype=jnp.int32)
    segment = (places >= first_end).astype(jnp.int32) + (places >= second_end).astype(jnp.int32)
    starts = jnp.where(segment == 0, 0, jnp.where(segment == 1, first_end, second_end))
    return (segment, places - starts)


def rotary_tables(position):
    half_width = HEAD // 2
    frequency = jnp.exp(
        jnp.arange(half_width, dtype=jnp.float32) * (-2.0 * math.log(10000.0) / HEAD)
    )
    angles = position.astype(jnp.float32)[:, None] * frequency[None, :]
    return (jnp.cos(angles)[:, None, :], jnp.sin(angles)[:, None, :])


def rotate(vectors, cosine, sine_table):
    half_width = vectors.shape[-1] // 2
    former = vectors[..., :half_width]
    latter = vectors[..., half_width:]
    return jnp.concatenate(
        [former * cosine - latter * sine_table, latter * cosine + former * sine_table], axis=-1
    )


def unrotate(gradient, cosine, sine_table):
    half_width = gradient.shape[-1] // 2
    former = gradient[..., :half_width]
    latter = gradient[..., half_width:]
    return jnp.concatenate(
        [former * cosine + latter * sine_table, latter * cosine - former * sine_table], axis=-1
    )


def norm_rows(values, gain_vector):
    centred = values - jnp.mean(values, axis=-1, keepdims=True)
    variance = jnp.mean(centred * centred, axis=-1, keepdims=True)
    return centred * lax.rsqrt(variance + EPSILON) * gain_vector


def block_allowed(query_segment, query_places, key_segment, key_place):
    return (query_segment[:, None] == key_segment[None, :]) & (
        key_place[None, :] <= query_places[:, None]
    )


def block_scores(queries, key_block, allowed):
    scores = jnp.einsum(
        "qhd,khd->hqk", queries, key_block, preferred_element_type=jnp.float32
    ) * HEAD ** (-0.5)
    return jnp.where(allowed[None], scores, MASKED)


def block_probs(queries, key_block, allowed, row_max, row_sum):
    scores = block_scores(queries, key_block, allowed)
    return jnp.where(allowed[None], jnp.exp(scores - row_max[..., None]) / row_sum[..., None], 0.0)


def softmax_stats(queries, key_blocks, layout_parts):
    query_segment, query_places, key_segments, key_places = layout_parts
    row_count, head_count = (queries.shape[0], queries.shape[1])
    start_state = (
        jnp.full((head_count, row_count), MASKED, jnp.float32),
        jnp.zeros((head_count, row_count), jnp.float32),
    )

    def advance(state, block_inputs):
        key_block, key_segment, key_place = block_inputs
        allowed = block_allowed(query_segment, query_places, key_segment, key_place)

        def update(current):
            row_max, row_sum = current
            scores = block_scores(queries, key_block, allowed)
            new_max = jnp.maximum(row_max, jnp.max(scores, axis=-1))
            weights = jnp.where(allowed[None], jnp.exp(scores - new_max[..., None]), 0.0)
            return (new_max, row_sum * jnp.exp(row_max - new_max) + jnp.sum(weights, axis=-1))

        return (lax.cond(jnp.any(allowed), update, lambda current: current, state), None)

    final_state, unused = lax.scan(advance, start_state, (key_blocks, key_segments, key_places))
    return final_state


def attention_output(queries, key_blocks, value_blocks, layout_parts, row_max, row_sum):
    query_segment, query_places, key_segments, key_places = layout_parts

    def advance(accum, block_inputs):
        key_block, value_block, key_segment, key_place = block_inputs
        allowed = block_allowed(query_segment, query_places, key_segment, key_place)

        def update(current):
            probs = block_probs(queries, key_block, allowed, row_max, row_sum).astype(jnp.bfloat16)
            return current + jnp.einsum(
                "hqk,khd->qhd", probs, value_block, preferred_element_type=jnp.float32
            )

        return (lax.cond(jnp.any(allowed), update, lambda current: current, accum), None)

    attended, unused = lax.scan(
        advance,
        jnp.zeros(queries.shape, jnp.float32),
        (key_blocks, value_blocks, key_segments, key_places),
    )
    return attended


def attention_backward(
    queries, grad_attended, delta_rows, key_blocks, value_blocks, layout_parts, row_max, row_sum
):
    query_segment, query_places, key_segments, key_places = layout_parts
    score_scale = HEAD ** (-0.5)

    def advance(grad_query, block_inputs):
        key_block, value_block, key_segment, key_place = block_inputs
        allowed = block_allowed(query_segment, query_places, key_segment, key_place)

        def update(current):
            probs = block_probs(queries, key_block, allowed, row_max, row_sum)
            grad_probs = jnp.einsum(
                "qhd,khd->hqk", grad_attended, value_block, preferred_element_type=jnp.float32
            )
            grad_scores = (probs * (grad_probs - delta_rows[..., None])).astype(jnp.bfloat16)
            new_query = (
                current
                + jnp.einsum(
                    "hqk,khd->qhd", grad_scores, key_block, preferred_element_type=jnp.float32
                )
                * score_scale
            )
            return (new_query, ())

        def bypass(current):
            return (current, ())

        return lax.cond(jnp.any(allowed), update, bypass, grad_query)

    grad_query, terms = lax.scan(
        advance,
        jnp.zeros(queries.shape, jnp.float32),
        (key_blocks, value_blocks, key_segments, key_places),
    )
    return (grad_query, None, None)


def project_front(inputs, triple_full, gain_full, cosine, sine_table):
    row_count, width = inputs.shape
    normed = norm_rows(inputs, gain_full.astype(jnp.float32)).astype(jnp.bfloat16)
    mixed = jnp.dot(normed, triple_full, preferred_element_type=jnp.float32)
    queries = rotate(mixed[:, :width].reshape(row_count, HEADS, HEAD), cosine, sine_table).astype(
        jnp.bfloat16
    )
    keys_local = (
        rotate(mixed[:, width : 2 * width].reshape(row_count, HEADS, HEAD), cosine, sine_table)
        .astype(jnp.bfloat16)
        .reshape(row_count, width)
    )
    values_local = mixed[:, 2 * width :].astype(jnp.bfloat16)
    return (normed, queries, keys_local, values_local)


def run_attention(queries, gathered, layout_parts):
    block_count = layout_parts[2].shape[0]
    key_blocks = gathered[0].reshape(block_count, -1, HEADS, HEAD)
    value_blocks = gathered[1].reshape(block_count, -1, HEADS, HEAD)
    row_max, row_sum = softmax_stats(queries, key_blocks, layout_parts)
    attended = attention_output(queries, key_blocks, value_blocks, layout_parts, row_max, row_sum)
    return (attended, key_blocks, value_blocks, row_max, row_sum)


def finish_layer(inputs, attended, output_full, up_full, down_full, second_full):
    row_count, width = inputs.shape
    attended_low = attended.reshape(row_count, width).astype(jnp.bfloat16)
    middle = inputs + jnp.dot(attended_low, output_full, preferred_element_type=jnp.float32)
    normed_two = norm_rows(middle, second_full.astype(jnp.float32)).astype(jnp.bfloat16)
    hidden = jnp.dot(normed_two, up_full, preferred_element_type=jnp.float32)
    activation = jax.nn.gelu(hidden).astype(jnp.bfloat16)
    result = middle + jnp.dot(activation, down_full, preferred_element_type=jnp.float32)
    return (result, attended_low, middle, normed_two, hidden, activation)


def whole_rows_body(
    tokens,
    triple_weight,
    output_weight,
    up_weight,
    down_weight,
    first_gain,
    second_gain,
    cotangent,
    frame_counts,
    text_counts,
    action_counts,
):
    row_count, width = tokens.shape
    pack_length = row_count * lax.axis_size("fsdp")
    first_place = lax.axis_index("fsdp") * row_count
    segment, position = clip_layout(frame_counts[0], text_counts[0], action_counts[0], pack_length)
    block_rows = min(1024, pack_length)
    block_count = pack_length // block_rows
    query_places = first_place + jnp.arange(row_count, dtype=jnp.int32)
    own_segment = lax.dynamic_slice_in_dim(segment, first_place, row_count, 0)
    layout_parts = (
        own_segment,
        query_places,
        segment.reshape(block_count, block_rows),
        jnp.arange(pack_length, dtype=jnp.int32).reshape(block_count, block_rows),
    )
    cosine, sine_table = rotary_tables(
        lax.dynamic_slice_in_dim(position, first_place, row_count, 0)
    )
    inputs = tokens.astype(jnp.float32)
    attention_set = (
        lax.all_gather(triple_weight, ("dp", "fsdp"), axis=0, tiled=True),
        lax.all_gather(output_weight, ("dp", "fsdp"), axis=0, tiled=True),
        lax.all_gather(first_gain, ("dp", "fsdp"), axis=0, tiled=True),
    )
    normed, queries, keys_local, values_local = project_front(
        inputs, attention_set[0], attention_set[2], cosine, sine_table
    )
    gathered = (
        lax.all_gather(keys_local, "fsdp", axis=0, tiled=True),
        lax.all_gather(values_local, "fsdp", axis=0, tiled=True),
    )
    attended, key_blocks, value_blocks, row_max, row_sum = run_attention(
        queries, gathered, layout_parts
    )
    feedforward_set = (
        lax.all_gather(up_weight, ("dp", "fsdp"), axis=0, tiled=True),
        lax.all_gather(down_weight, ("dp", "fsdp"), axis=0, tiled=True),
        lax.all_gather(second_gain, ("dp", "fsdp"), axis=0, tiled=True),
    )
    kept_parts = finish_layer(
        inputs,
        attended,
        attention_set[1],
        feedforward_set[0],
        feedforward_set[1],
        feedforward_set[2],
    )
    layer_output = kept_parts[0].astype(jnp.bfloat16)
    attention_set = (
        lax.all_gather(triple_weight, ("dp", "fsdp"), axis=0, tiled=True),
        lax.all_gather(output_weight, ("dp", "fsdp"), axis=0, tiled=True),
        lax.all_gather(first_gain, ("dp", "fsdp"), axis=0, tiled=True),
    )
    normed, queries, keys_local, values_local = project_front(
        inputs, attention_set[0], attention_set[2], cosine, sine_table
    )
    gathered = (
        lax.all_gather(keys_local, "fsdp", axis=0, tiled=True),
        lax.all_gather(values_local, "fsdp", axis=0, tiled=True),
    )
    attended, key_blocks, value_blocks, row_max, row_sum = run_attention(
        queries, gathered, layout_parts
    )
    feedforward_set = (
        lax.all_gather(up_weight, ("dp", "fsdp"), axis=0, tiled=True),
        lax.all_gather(down_weight, ("dp", "fsdp"), axis=0, tiled=True),
        lax.all_gather(second_gain, ("dp", "fsdp"), axis=0, tiled=True),
    )
    kept_parts = finish_layer(
        inputs,
        attended,
        attention_set[1],
        feedforward_set[0],
        feedforward_set[1],
        feedforward_set[2],
    )
    unused_result, attended_low, middle, normed_two, hidden, activation = kept_parts
    down_term = jnp.einsum("rf,rd->fd", activation, cotangent, preferred_element_type=jnp.float32)
    grad_activation = jnp.einsum(
        "rd,fd->rf", cotangent, feedforward_set[1], preferred_element_type=jnp.float32
    )
    unused_gelu, gelu_pull = jax.vjp(jax.nn.gelu, hidden)
    grad_hidden = gelu_pull(grad_activation)[0].astype(jnp.bfloat16)
    up_term = jnp.einsum("rd,rf->df", normed_two, grad_hidden, preferred_element_type=jnp.float32)
    grad_normed_two = jnp.einsum(
        "rf,df->rd", grad_hidden, feedforward_set[0], preferred_element_type=jnp.float32
    )
    unused_second, second_pull = jax.vjp(norm_rows, middle, feedforward_set[2].astype(jnp.float32))
    grad_middle_norm, second_gain_term = second_pull(grad_normed_two)
    grad_middle = cotangent.astype(jnp.float32) + grad_middle_norm
    feedforward_sums = (
        lax.psum_scatter(up_term, ("dp", "fsdp"), scatter_dimension=0, tiled=True),
        lax.psum_scatter(down_term, ("dp", "fsdp"), scatter_dimension=0, tiled=True),
        lax.psum_scatter(second_gain_term, ("dp", "fsdp"), scatter_dimension=0, tiled=True),
    )
    grad_branch = grad_middle.astype(jnp.bfloat16)
    output_term = jnp.einsum(
        "rd,re->de", attended_low, grad_branch, preferred_element_type=jnp.float32
    )
    grad_attended = (
        jnp.einsum("re,de->rd", grad_branch, attention_set[1], preferred_element_type=jnp.float32)
        .astype(jnp.bfloat16)
        .reshape(row_count, HEADS, HEAD)
    )
    delta_rows = jnp.sum(grad_attended.astype(jnp.float32) * attended, axis=-1).T
    score_scale = HEAD ** (-0.5)
    grad_query = attention_backward(
        queries, grad_attended, delta_rows, key_blocks, value_blocks, layout_parts, row_max, row_sum
    )[0]
    pack_stats = (
        lax.all_gather(row_max.T, "fsdp", axis=0, tiled=True),
        lax.all_gather(row_sum.T, "fsdp", axis=0, tiled=True),
        lax.all_gather(delta_rows.T, "fsdp", axis=0, tiled=True),
    )
    own_keys = keys_local.reshape(row_count, HEADS, HEAD)
    own_values = values_local.reshape(row_count, HEADS, HEAD)
    empty_grads = jnp.zeros((row_count, HEADS, HEAD), jnp.float32)
    query_piece = lax.all_gather(queries, "fsdp", axis=0, tiled=True)
    grad_piece = lax.all_gather(grad_attended, "fsdp", axis=0, tiled=True)
    piece_rows = query_piece.shape[0]
    block_size = min(1024, piece_rows)
    block_total = piece_rows // block_size

    def advance(current, block_index):
        offset = block_index * block_size
        query_part = lax.dynamic_slice_in_dim(query_piece, offset, block_size, 0)
        grad_part = lax.dynamic_slice_in_dim(grad_piece, offset, block_size, 0)
        max_part = lax.dynamic_slice_in_dim(pack_stats[0], offset, block_size, 0).T
        sum_part = lax.dynamic_slice_in_dim(pack_stats[1], offset, block_size, 0).T
        delta_part = lax.dynamic_slice_in_dim(pack_stats[2], offset, block_size, 0).T
        part_segment = lax.dynamic_slice_in_dim(segment, offset, block_size, 0)
        part_places = offset + jnp.arange(block_size, dtype=jnp.int32)
        allowed = block_allowed(part_segment, part_places, own_segment, query_places)

        def update(pair):
            probs = block_probs(query_part, own_keys, allowed, max_part, sum_part)
            grad_probs = jnp.einsum(
                "qhd,khd->hqk", grad_part, own_values, preferred_element_type=jnp.float32
            )
            grad_scores = (probs * (grad_probs - delta_part[..., None])).astype(jnp.bfloat16)
            grad_key = (
                pair[0]
                + jnp.einsum(
                    "hqk,qhd->khd", grad_scores, query_part, preferred_element_type=jnp.float32
                )
                * score_scale
            )
            grad_value = pair[1] + jnp.einsum(
                "hqk,qhd->khd",
                probs.astype(jnp.bfloat16),
                grad_part,
                preferred_element_type=jnp.float32,
            )
            return (grad_key, grad_value)

        return (lax.cond(jnp.any(allowed), update, lambda pair: pair, current), None)

    result, unused = lax.scan(
        advance, (empty_grads, empty_grads), jnp.arange(block_total, dtype=jnp.int32)
    )
    key_grad_sum = result[0].reshape(row_count, width)
    value_grad_sum = result[1].reshape(row_count, width)
    grad_query_full = (
        unrotate(grad_query, cosine, sine_table).reshape(row_count, width).astype(jnp.bfloat16)
    )
    grad_key_full = (
        unrotate(key_grad_sum.reshape(row_count, HEADS, HEAD), cosine, sine_table)
        .reshape(row_count, width)
        .astype(jnp.bfloat16)
    )
    grad_value_full = value_grad_sum.astype(jnp.bfloat16)
    grad_mixed = jnp.concatenate([grad_query_full, grad_key_full, grad_value_full], axis=1)
    triple_term = jnp.einsum("rd,re->de", normed, grad_mixed, preferred_element_type=jnp.float32)
    grad_normed = jnp.einsum(
        "re,de->rd", grad_mixed, attention_set[0], preferred_element_type=jnp.float32
    )
    unused_first, first_pull = jax.vjp(norm_rows, inputs, attention_set[2].astype(jnp.float32))
    grad_input_norm, first_gain_term = first_pull(grad_normed)
    token_grad = (grad_middle + grad_input_norm).astype(jnp.bfloat16)
    attention_sums = (
        lax.psum_scatter(triple_term, ("dp", "fsdp"), scatter_dimension=0, tiled=True),
        lax.psum_scatter(output_term, ("dp", "fsdp"), scatter_dimension=0, tiled=True),
        lax.psum_scatter(first_gain_term, ("dp", "fsdp"), scatter_dimension=0, tiled=True),
    )
    return (
        layer_output,
        token_grad,
        attention_sums[0],
        attention_sums[1],
        feedforward_sums[0],
        feedforward_sums[1],
        attention_sums[2],
        feedforward_sums[2],
    )


AXES = ("dp", "fsdp")
DEVICES = 32
MEMBERS = 8
CORE, ZL, Y = 8, 2, 1
X, ZH = 16, 4
BF16 = jnp.bfloat16
F32 = jnp.float32
SMEM = pl.BlockSpec(memory_space=pltpu.SMEM)
VMEM = pl.BlockSpec(memory_space=pltpu.VMEM)
HBM = pl.BlockSpec(memory_space=pltpu.HBM)


def swap(array, bits):
    return lax.ppermute(array, AXES, [(i, i ^ bits) for i in range(DEVICES)])


def alike(*bits):
    groups = {}
    for i in range(DEVICES):
        groups.setdefault(i & ~sum(bits), []).append(i)
    return list(groups.values())


def exchange(array, *bits):
    return lax.all_to_all(array, AXES, 0, 0, tiled=True, axis_index_groups=alike(*bits))


def after(array, *others):
    return lax.optimization_barrier((array,) + others)[0]


def together(*arrays):
    return lax.optimization_barrier(arrays)


def regroup_pairs():
    def target(i):
        x, core, zh, low = i >> 4, (i >> 3) & 1, (i >> 2) & 1, i & 3
        return (x << 4) | (zh << 3) | (core << 2) | low

    return [(i, target(i)) for i in range(DEVICES)]


def regroup(array):
    return lax.ppermute(array, AXES, regroup_pairs())


def turn_pairs():
    return [(i, (i & 14) | (i & 1) << 4 | i >> 4) for i in range(DEVICES)]


def gather(own, *bits):
    return lax.all_gather(own, AXES, axis=0, tiled=True, axis_index_groups=alike(*bits))


def collect(parts):
    return exchange(parts.reshape(4, -1, parts.shape[1]), ZL, Y)


def row_product(half, left, right, transposed, came=None):
    count, depth = left.shape[0] // 2, left.shape[1]
    width = right.shape[0] if transposed else right.shape[1]
    tile = 512

    def kernel(half_ref, left_ref, right_ref, *rest):
        if transposed:
            total = dot_transposed(left_ref[...], right_ref[...])
        else:
            total = jnp.dot(left_ref[...], right_ref[...], preferred_element_type=F32)
        if came is not None:
            total = total + rest[0][...].astype(F32)
        rest[-1][...] = total.astype(BF16)

    columns = pl.BlockSpec((count, tile), lambda i, half_ref: (0, i))
    if transposed:
        right_spec = pl.BlockSpec((tile, depth), lambda i, half_ref: (i, 0))
    else:
        right_spec = pl.BlockSpec((depth, tile), lambda i, half_ref: (0, i))
    more = [] if came is None else [came]
    return pl.pallas_call(
        kernel,
        grid_spec=pltpu.PrefetchScalarGridSpec(
            num_scalar_prefetch=1,
            grid=(width // tile,),
            in_specs=[pl.BlockSpec((count, depth), lambda i, half_ref: (half_ref[0], 0)), right_spec]
            + [columns] * len(more),
            out_specs=columns,
        ),
        out_shape=jax.ShapeDtypeStruct((count, width), BF16),
        compiler_params=pltpu.CompilerParams(vmem_limit_bytes=32 << 20),
    )(half, left, right, *more)


def product_sums(core, rows, right, transposed=False):
    near, far = core.reshape(1), (1 - core).reshape(1)
    came = swap(row_product(far, rows, right, transposed), CORE)
    return row_product(near, rows, right, transposed, came)


def hidden_columns(member, width):
    core, zl, y = (member >> 2) & 1, (member >> 1) & 1, member & 1
    return [
        ((gx * X + core * CORE + gz * ZH + zl * ZL + y) * width, width)
        for gx in range(2)
        for gz in range(2)
    ]


def head_columns(member, width):
    core, zl, y = (member >> 2) & 1, (member >> 1) & 1, member & 1
    return [
        (part * width + ((y * 2 + core) * 4 + half * 2 + zl) * HEAD, HEAD)
        for part in range(3)
        for half in range(2)
    ]


def deal_columns(own, columns, extra=()):
    rows = own.shape[0]
    width = own.shape[1] // MEMBERS
    more = 16 if extra else 0

    def kernel(*refs):
        own_ref, slabs_ref = refs[0], refs[-1]
        for member in range(MEMBERS):
            start = 0
            for place, size in columns(member):
                slabs_ref[member, :rows, start : start + size] = own_ref[:, place : place + size]
                start += size
            if more:
                slabs_ref[member, rows:, :] = jnp.zeros((more, width), own.dtype)
                for i, extra_ref in enumerate(refs[1:-1]):
                    slabs_ref[member, rows:, i * HEAD : i * HEAD + rows] = jnp.broadcast_to(
                        extra_ref[...], (more, rows)
                    )

    arrays = [own, *extra]
    return pl.pallas_call(
        kernel,
        out_shape=jax.ShapeDtypeStruct((MEMBERS, rows + more, width), own.dtype),
        in_specs=[VMEM] * len(arrays),
        out_specs=VMEM,
    )(*arrays)


def pair_up(index, mine, theirs):
    return jnp.where(index == 0, jnp.stack([mine, theirs]), jnp.stack([theirs, mine]))


def row_copies(places_ref, pieces, whole_ref, sems, rows):
    sources = [(piece, start) for piece in pieces for start in range(0, piece.shape[0], rows)]
    return [
        pltpu.make_async_copy(
            piece.at[pl.ds(start, rows)],
            whole_ref.at[pl.ds(pl.multiple_of(places_ref[n] * rows, rows), rows)],
            sems.at[n],
        )
        for n, (piece, start) in enumerate(sources)
    ]


def place_rows(places, pieces, rows):
    count = sum(piece.shape[0] for piece in pieces)

    def kernel(places_ref, *rest):
        whole_ref, sems = rest[-2:]
        copies = row_copies(places_ref, rest[:-2], whole_ref, sems, rows)
        for copy in copies:
            copy.start()
        for copy in copies:
            copy.wait()

    return pl.pallas_call(
        kernel,
        out_shape=jax.ShapeDtypeStruct((count, pieces[0].shape[1]), BF16),
        in_specs=[SMEM] + [HBM] * len(pieces),
        out_specs=VMEM,
        scratch_shapes=[pltpu.SemaphoreType.DMA((count // rows,))],
        compiler_params=pltpu.CompilerParams(vmem_limit_bytes=16 << 20),
    )(places, *pieces)


def place_columns(slabs, own, gain, columns):
    rows = own.shape[0]
    sources = [(i, lane) for i, slab in enumerate(slabs) for lane in range(0, slab.shape[2], HEAD)]

    def kernel(*refs):
        slab_refs, (own_ref, gain_ref, whole_ref, sum_ref) = refs[: len(slabs)], refs[len(slabs) :]
        total = jnp.zeros((rows, HEAD), F32)
        for member in range(MEMBERS):
            places = [place + lane for place, size in columns(member) for lane in range(0, size, HEAD)]
            for place, (i, lane) in zip(places, sources):
                part = slab_refs[i][member, :, lane : lane + HEAD].astype(F32)
                whole_ref[:, place : place + HEAD] = part
                total = total + part * own_ref[:, place : place + HEAD].astype(F32)
        sum_ref[...] = jnp.sum(total, axis=1, keepdims=True) / gain_ref[...]

    return pl.pallas_call(
        kernel,
        out_shape=[jax.ShapeDtypeStruct(own.shape, F32), jax.ShapeDtypeStruct((rows, 1), F32)],
        in_specs=[VMEM] * (len(slabs) + 2),
        out_specs=[VMEM] * 2,
        compiler_params=pltpu.CompilerParams(vmem_limit_bytes=32 << 20),
    )(*slabs, own, gain)


def give(index, bits, grad):
    return swap(lax.dynamic_index_in_dim(grad, 1 - index, 0, False), bits)


def half_sum(first, second, grad, came):
    outer, inner, width = grad.shape[1], grad.shape[3], grad.shape[4]
    mine = lax.dynamic_slice(grad, (first, 0, second, 0, 0), (1, outer, 1, inner, width))
    theirs = lax.dynamic_slice(came, (0, second, 0, 0), (outer, 1, inner, width))
    shape = (outer, inner, width)
    return mine.reshape(shape).astype(F32) + theirs.reshape(shape).astype(F32)


def give_sum(first, second, bits, grad, came):
    return swap(half_sum(first, 1 - second, grad, came).astype(BF16), bits)


def keep_sum(first, second, grad, came, far):
    return half_sum(first, second, grad, came) + far.astype(F32)


def turn(vectors, cosine, sine):
    return vectors * cosine + pltpu.roll(vectors, HEAD // 2, 1) * sine


def block_mask(ends_ref, block):
    first_end, second_end = ends_ref[0], ends_ref[1]
    place = lax.broadcasted_iota(jnp.int32, (BLOCK, 1), 0) + block * BLOCK
    key_place = lax.broadcasted_iota(jnp.int32, (1, (block + 1) * BLOCK), 1)
    start = jnp.where(place < first_end, 0, jnp.where(place < second_end, first_end, second_end))
    return (key_place <= place) & (key_place >= start)


def masked_probs(queries, keys, allowed):
    scores = lax.dot_general(queries, keys, (((1,), (1,)), ((), ())), preferred_element_type=F32)
    scores = jnp.where(allowed, scores * HEAD ** (-0.5), MASKED)
    weights = jnp.exp(scores - jnp.max(scores, axis=-1, keepdims=True))
    return weights * (1.0 / jnp.sum(weights, axis=-1, keepdims=True))


BLOCK = 256


def attention_forward(ends, places, normal, pieces, cosine, sine):
    count, depth = normal.shape
    width = pieces[0].shape[1] // 3
    block_rows = depth // 8

    def kernel(ends_ref, places_ref, normal_ref, cos_ref, sin_ref, *rest):
        piece_refs, (q_ref, k_ref, v_ref, out_ref, weight_ref, sems) = rest[: len(pieces)], rest[len(pieces) :]
        copies = row_copies(places_ref, piece_refs, weight_ref, sems, block_rows)
        for copy in copies:
            copy.start()
        for copy in copies:
            copy.wait()

        @pl.loop(0, count // BLOCK)
        def _(block):
            here = pl.ds(pl.multiple_of(block * BLOCK, BLOCK), BLOCK)
            mixed = jnp.dot(normal_ref[here, :], weight_ref[...], preferred_element_type=F32)
            cos, sin = cos_ref[here, :], sin_ref[here, :]
            v_ref[here, :] = mixed[:, 2 * width :].astype(BF16)
            for head in range(width // HEAD):
                span = slice(head * HEAD, (head + 1) * HEAD)
                key_span = slice(width + head * HEAD, width + (head + 1) * HEAD)
                q_ref[here, span] = turn(mixed[:, span], cos, sin).astype(BF16)
                k_ref[here, span] = turn(mixed[:, key_span], cos, sin).astype(BF16)

        for block in range(count // BLOCK):
            here, keys = slice(block * BLOCK, (block + 1) * BLOCK), slice(0, (block + 1) * BLOCK)
            allowed = block_mask(ends_ref, block)
            for head in range(width // HEAD):
                span = slice(head * HEAD, (head + 1) * HEAD)
                probs = masked_probs(q_ref[here, span], k_ref[keys, span], allowed)
                out_ref[here, span] = jnp.dot(
                    probs.astype(BF16), v_ref[keys, span], preferred_element_type=F32
                ).astype(BF16)

    return pl.pallas_call(
        kernel,
        out_shape=[jax.ShapeDtypeStruct((count, width), BF16)] * 4
        + [jax.ShapeDtypeStruct((depth, 3 * width), BF16)],
        in_specs=[SMEM] * 2 + [VMEM] * 3 + [HBM] * len(pieces),
        out_specs=[VMEM] * 5,
        scratch_shapes=[pltpu.SemaphoreType.DMA((8,))],
        compiler_params=pltpu.CompilerParams(vmem_limit_bytes=48 << 20),
    )(ends, places, normal, cosine, sine, *pieces)


def attention_backward_heads(ends, queries, keys, values, grad_out, cosine, sine):
    count, width = queries.shape

    def kernel(ends_ref, q_ref, k_ref, v_ref, g_ref, cos_ref, sin_ref, out_ref, gk_ref, gv_ref):
        gk_ref[...] = jnp.zeros_like(gk_ref)
        gv_ref[...] = jnp.zeros_like(gv_ref)

        for block in range(count // BLOCK):
            here, keys = slice(block * BLOCK, (block + 1) * BLOCK), slice(0, (block + 1) * BLOCK)
            allowed = block_mask(ends_ref, block)
            for head in range(width // HEAD):
                span = slice(head * HEAD, (head + 1) * HEAD)
                q, g = q_ref[here, span], g_ref[here, span]
                probs = masked_probs(q, k_ref[keys, span], allowed)
                grad_probs = lax.dot_general(
                    g, v_ref[keys, span], (((1,), (1,)), ((), ())), preferred_element_type=F32
                )
                delta = jnp.sum(probs * grad_probs, axis=-1, keepdims=True)
                grad_scores = (probs * (grad_probs - delta)).astype(BF16)
                grad_query = jnp.dot(grad_scores, k_ref[keys, span], preferred_element_type=F32)
                out_ref[here, span] = turn(
                    grad_query * HEAD ** (-0.5), cos_ref[here, :], -sin_ref[here, :]
                ).astype(BF16)
                over_rows = (((0,), (0,)), ((), ()))
                gk_ref[keys, span] += lax.dot_general(grad_scores, q, over_rows, preferred_element_type=F32)
                gv_ref[keys, span] += lax.dot_general(
                    probs.astype(BF16), g, over_rows, preferred_element_type=F32
                )

        out_ref[:, 2 * width :] = gv_ref[...].astype(BF16)
        for head in range(width // HEAD):
            span = slice(head * HEAD, (head + 1) * HEAD)
            out_ref[:, width + head * HEAD : width + (head + 1) * HEAD] = turn(
                gk_ref[:, span] * HEAD ** (-0.5), cos_ref[...], -sin_ref[...]
            ).astype(BF16)

    return pl.pallas_call(
        kernel,
        out_shape=jax.ShapeDtypeStruct((count, 3 * width), BF16),
        in_specs=[SMEM] + [VMEM] * 6,
        out_specs=VMEM,
        scratch_shapes=[pltpu.VMEM((count, width), F32), pltpu.VMEM((count, width), F32)],
        compiler_params=pltpu.CompilerParams(vmem_limit_bytes=48 << 20),
    )(ends, queries, keys, values, grad_out, cosine, sine)


def norm_parts(values):
    centred = values - jnp.mean(values, axis=-1, keepdims=True)
    inverse = lax.rsqrt(jnp.mean(centred * centred, axis=-1, keepdims=True) + EPSILON)
    return centred * inverse, inverse


def norm_backward(values, scaled):
    normal, inverse = norm_parts(values)
    return inverse * (
        scaled
        - jnp.mean(scaled, axis=-1, keepdims=True)
        - normal * jnp.mean(scaled * normal, axis=-1, keepdims=True)
    )


ROWS = 64


def norm_of(values, gain):
    def kernel(values_ref, gain_ref, out_ref):
        out_ref[...] = (norm_parts(values_ref[...].astype(F32))[0] * gain_ref[...]).astype(BF16)

    count, width = values.shape
    return pl.pallas_call(
        kernel,
        grid=(count // ROWS,),
        out_shape=jax.ShapeDtypeStruct(values.shape, BF16),
        in_specs=[pl.BlockSpec((ROWS, width), lambda i: (i, 0)), pl.BlockSpec((1, width), lambda i: (0, 0))],
        out_specs=pl.BlockSpec((ROWS, width), lambda i: (i, 0)),
    )(values, gain)


def row_kernel(kernel, parts, arrays, gain, outs):
    rows, width = parts.shape[1:]
    whole = pl.BlockSpec((4, ROWS, width), lambda i: (0, i, 0))
    single = pl.BlockSpec((ROWS, width), lambda i: (i, 0))
    return pl.pallas_call(
        kernel,
        grid=(rows // ROWS,),
        out_shape=[jax.ShapeDtypeStruct((rows, width), kind) for kind in outs],
        in_specs=[whole] + [single] * len(arrays) + [pl.BlockSpec((1, width), lambda i: (0, 0))],
        out_specs=[single] * len(outs),
    )(parts, *arrays, gain)


def add_parts(parts_ref):
    total = parts_ref[0].astype(F32)
    for i in range(1, 4):
        total = total + parts_ref[i].astype(F32)
    return total


def middle_rows(parts, inputs, gain):
    def kernel(parts_ref, inputs_ref, gain_ref, middle_ref, normal_ref):
        middle = inputs_ref[...].astype(F32) + add_parts(parts_ref)
        middle_ref[...] = middle
        normal_ref[...] = (norm_parts(middle)[0] * gain_ref[...]).astype(BF16)

    return row_kernel(kernel, parts, [inputs], gain, [F32, BF16])


def grad_middle_rows(parts, middle, cotangent, gain):
    def kernel(parts_ref, middle_ref, cotangent_ref, gain_ref, grad_ref, branch_ref):
        grad = cotangent_ref[...].astype(F32) + norm_backward(middle_ref[...], add_parts(parts_ref) * gain_ref[...])
        grad_ref[...] = grad
        branch_ref[...] = grad.astype(BF16)

    return row_kernel(kernel, parts, [middle, cotangent], gain, [F32, BF16])


def token_grad_rows(parts, inputs, grad_middle, gain):
    def kernel(parts_ref, inputs_ref, middle_ref, gain_ref, grad_ref):
        grad = norm_backward(inputs_ref[...].astype(F32), add_parts(parts_ref) * gain_ref[...])
        grad_ref[...] = (middle_ref[...] + grad).astype(BF16)

    return row_kernel(kernel, parts, [inputs, grad_middle], gain, [BF16])[0]


def feed_forward(normal, grad_activation, places, pieces, piece_rows):
    count, width = normal.shape
    hidden_width = pieces[0].shape[1]
    step_rows = 256
    steps = count // step_rows

    def kernel(places_ref, normal_ref, grad_activation_ref, *rest):
        act_ref, grad_ref, up_out, up_ref, sems, out_sem = rest[len(pieces) :]
        step = pl.program_id(0)
        copies = row_copies(places_ref, rest[: len(pieces)], up_ref, sems, piece_rows)
        back = pltpu.make_async_copy(up_ref, up_out, out_sem)

        @pl.when(step == 0)
        def _():
            for copy in copies:
                copy.start()
            for copy in copies:
                copy.wait()
            back.start()

        hidden = jnp.dot(normal_ref[...], up_ref[...], preferred_element_type=F32)
        scale = math.sqrt(2.0 / math.pi)
        square = hidden * hidden
        tanh = jnp.tanh(scale * hidden * (1.0 + 0.044715 * square))
        act_ref[...] = (0.5 * hidden * (1.0 + tanh)).astype(BF16)
        slope = 0.5 * (1.0 + tanh) + (0.5 * scale) * hidden * (1.0 - tanh * tanh) * (
            1.0 + (3.0 * 0.044715) * square
        )
        grad_ref[...] = (grad_activation_ref[...] * slope).astype(BF16)

        @pl.when(step == steps - 1)
        def _():
            back.wait()

    row_spec = pl.BlockSpec((step_rows, width), lambda i: (i, 0))
    hidden_spec = pl.BlockSpec((step_rows, hidden_width), lambda i: (i, 0))
    return pl.pallas_call(
        kernel,
        grid=(steps,),
        out_shape=[jax.ShapeDtypeStruct((count, hidden_width), BF16)] * 2
        + [jax.ShapeDtypeStruct((width, hidden_width), BF16)],
        in_specs=[SMEM, row_spec, hidden_spec] + [HBM] * len(pieces),
        out_specs=[hidden_spec, hidden_spec, HBM],
        scratch_shapes=[
            pltpu.VMEM((width, hidden_width), BF16),
            pltpu.SemaphoreType.DMA((width // piece_rows,)),
            pltpu.SemaphoreType.DMA,
        ],
        compiler_params=pltpu.CompilerParams(vmem_limit_bytes=48 << 20),
    )(places, normal, grad_activation, *pieces)


def contract_rows(left, right):
    return lax.dot_general(left, right, (((0,), (0,)), ((), ())), preferred_element_type=F32)


def dot_transposed(left, right):
    return lax.dot_general(left, right, (((1,), (1,)), ((), ())), preferred_element_type=F32)


class Step:
    def __init__(self, function, *needs):
        self.function, self.needs, self.made = function, needs, None

    def get(self):
        if self.made is None:
            self.put(self.function(*[need.get() for need in self.needs]))
        return self.made[0]

    def put(self, value):
        self.made = (value,)


def grouped_body(
    tokens_own,
    triple_weight,
    output_weight,
    up_weight,
    down_weight,
    first_gain,
    second_gain,
    cotangent_own,
    frame_counts,
    text_counts,
    action_counts,
):
    rows, width = tokens_own.shape
    count = rows * MEMBERS
    dp, fsdp = lax.axis_index("dp"), lax.axis_index("fsdp")
    x, core = dp >> 1, dp & 1
    zh = fsdp >> 2

    counts = jnp.concatenate(
        [frame_counts.reshape(-1), text_counts.reshape(-1), action_counts.reshape(-1)]
    )
    counts = jnp.where(core == zh, counts, swap(counts, CORE))
    frames = counts[:2]
    slots = text_counts.shape[-1]
    texts = counts[2 : 2 + 2 * slots].reshape(2, slots)
    actions = counts[2 + 2 * slots :].reshape(2, slots)
    live = jnp.arange(slots, dtype=jnp.int32) < frames[:, None]
    lengths = jnp.sum(jnp.where(live, IMG + texts + actions, 0), axis=-1)
    first_end = lengths[0]
    second_end = lengths[0] + lengths[1]
    pack_ends = jnp.stack([first_end, second_end]).astype(jnp.int32)
    places = jnp.arange(count, dtype=jnp.int32)
    starts = jnp.where(places < first_end, 0, jnp.where(places < second_end, first_end, second_end))
    cosine_table, sine_table = rotary_tables(places - starts)
    cosine_table = jnp.concatenate([cosine_table[:, 0], cosine_table[:, 0]], axis=1)
    sine_table = jnp.concatenate([-sine_table[:, 0], sine_table[:, 0]], axis=1)

    sides = ((0, 0), (0, 1), (1, 0), (1, 1))
    rows_of_weight = triple_weight.shape[0]
    block = rows_of_weight * 4
    quarter = down_weight.shape[0] // 4
    hidden_width = up_weight.shape[1] // DEVICES
    triple_columns = lambda m: head_columns(m, width)
    up_columns = lambda m: hidden_columns(m, hidden_width)
    first_column = first_gain.astype(F32)[:, None]
    second_column = second_gain.astype(F32)[:, None]

    def places_of(pieces):
        return jnp.stack([place for a, b, parts in pieces for place in parts(x ^ a, zh ^ b)]).astype(jnp.int32)

    def column_places(*which):
        return lambda sx, sz: [sx * 4 + c * 2 + sz for c in which]

    def down_places(*which):
        return lambda sx, sz: [(sx * 2 + sz) * 4 + q for q in which]

    tokens, cotangent = Step(lambda: tokens_own), Step(lambda: cotangent_own)
    down_own, output_own = Step(lambda: down_weight), Step(lambda: output_weight)
    ends, cosine, sine = Step(lambda: pack_ends), Step(lambda: cosine_table), Step(lambda: sine_table)

    triple_dealt = Step(lambda: deal_columns(triple_weight, triple_columns, [first_gain[None], second_gain[None]]))
    triple_all = Step(lambda a: exchange(a, CORE, ZL, Y), triple_dealt)
    triple_own = Step(lambda a: a[:, :rows_of_weight].reshape(-1, a.shape[-1]), triple_all)
    triple_x = Step(lambda a: swap(a, X), triple_own)
    triple_half = [Step(lambda a, h=h: a[h * block : (h + 1) * block], triple_own) for h in range(2)]
    triple_zh = [Step(lambda a: swap(a, ZH), half) for half in triple_half]
    triple_xz = [Step(lambda a: swap(a, X), half) for half in triple_zh]
    inputs = Step(regroup, tokens)
    all_inputs = Step(lambda a: gather(a, CORE, ZL, Y), inputs)
    gains_own = Step(
        lambda a: jnp.concatenate(
            [a[:, rows_of_weight, i * HEAD : i * HEAD + rows_of_weight] for i in range(2)], axis=1
        ),
        triple_all,
    )
    gains_pair = Step(lambda a: pair_up(zh, a, swap(a, ZH)), gains_own)

    def whole_gains(pair):
        whole = pair_up(x, pair, swap(pair, X)).reshape(2, 2, 2, 4, 2, -1)
        return whole.transpose(4, 0, 2, 1, 3, 5).reshape(2, -1).astype(F32)

    gains = Step(whole_gains, gains_pair)
    normal = Step(lambda a, gains: norm_of(a, gains[:1]), all_inputs, gains)
    own_cotangent = Step(regroup, cotangent)
    all_cotangent = Step(lambda a: gather(a, CORE, ZL, Y), own_cotangent)
    turned = Step(lambda a: lax.ppermute(a, AXES, turn_pairs()), output_own)
    turned_zh = Step(lambda a: swap(a, ZH), turned)
    turned_pair = Step(lambda a, b: pair_up(zh, a, b), turned, turned_zh)
    turned_x = Step(lambda a: swap(a, X), turned_pair)

    def whole_output(pair, pair_x):
        whole = jnp.where(x == 0, jnp.stack([pair, pair_x], axis=1), jnp.stack([pair_x, pair], axis=1))
        return whole.reshape(-1, width)

    output = Step(whole_output, turned_pair, turned_x)
    down_x = Step(lambda a: swap(a, X), down_own)
    down_part = [Step(lambda a, q=q: a[q * quarter : (q + 1) * quarter], down_own) for q in range(4)]
    down_zh = [Step(lambda a: swap(a, ZH), part) for part in down_part]
    down_xz = [Step(lambda a: swap(a, X), part) for part in down_zh]

    def whole_down(own, own_x, *rest):
        places = [(0, 0, down_places(0, 1, 2, 3)), (1, 0, down_places(0, 1, 2, 3))]
        places += [(0, 1, down_places(q)) for q in range(4)] + [(1, 1, down_places(q)) for q in range(4)]
        return place_rows(places_of(places), [own, own_x, *rest], quarter)

    down = Step(whole_down, down_own, down_x, *down_zh, *down_xz)
    grad_activation = Step(dot_transposed, all_cotangent, down)
    up_dealt = Step(lambda: deal_columns(up_weight, up_columns))
    up_own = Step(lambda a: exchange(a, CORE, ZL, Y).reshape(-1, a.shape[-1]), up_dealt)
    up_x = Step(lambda a: swap(a, X), up_own)
    up_half = [Step(lambda a, h=h: a[h * block : (h + 1) * block], up_own) for h in range(2)]
    up_zh = [Step(lambda a: swap(a, ZH), half) for half in up_half]
    up_xz = [Step(lambda a: swap(a, X), half) for half in up_zh]

    halved = [(0, 0, column_places(0, 1)), (0, 1, column_places(0)), (0, 1, column_places(1))]
    halved += [(1, 0, column_places(0, 1)), (1, 1, column_places(0)), (1, 1, column_places(1))]

    def attend(ends, normal, cosine, sine, *pieces):
        return attention_forward(ends, places_of(halved), normal, list(pieces), cosine, sine)

    attention = Step(attend, ends, normal, cosine, sine, triple_own, *triple_zh, triple_x, *triple_xz)
    attended_partial = Step(lambda a, output: product_sums(core, a[3], output), attention, output)
    attended_sums = Step(collect, attended_partial)
    middle = Step(lambda a, inputs, gains: middle_rows(a, inputs, gains[1:]), attended_sums, inputs, gains)
    normal_two = Step(lambda a: gather(a[1], CORE, ZL, Y), middle)

    def feed(normal_two, grad_activation, *pieces):
        return feed_forward(normal_two, grad_activation, places_of(halved), list(pieces), block)

    forward = Step(feed, normal_two, grad_activation, up_own, *up_zh, up_x, *up_xz)

    def columns(left, right, start, stop, shape):
        return contract_rows(left, right[:, start:stop]).astype(BF16).reshape(*shape, -1, stop - start)

    class Reduction:
        def __init__(self, kept, one, two, sent=None, index=None):
            (side, bits), (other, other_bits) = one, two
            index = side if index is None else index
            self.kept = kept
            self.sent = sent or Step(lambda a: lax.dynamic_index_in_dim(a, 1 - side, 0, False), kept)
            self.came = Step(lambda a: swap(a, bits), self.sent)
            self.half = Step(lambda a, came: half_sum(index, 1 - other, a, came).astype(BF16), kept, self.came)
            self.far = Step(lambda a: swap(a, other_bits), self.half)
            self.total = Step(lambda a, came, far: keep_sum(index, other, a, came, far), kept, self.came, self.far)

    over_x, over_zh = (x, X), (zh, ZH)

    def x_first(left, right, pick, start, lanes, shape):
        def side(index):
            def product(a, b):
                whole, columns_of = pick(a, b)
                half = whole.shape[1] // 2
                own = lax.dynamic_slice_in_dim(whole, index * half, half, 1)
                return columns(own, columns_of, start * HEAD, (start + lanes) * HEAD, (1,) + shape)

            return product

        sent = Step(lambda a, b: side(1 - x)(a, b)[0], left, right)
        return Reduction(Step(side(x), left, right), over_x, over_zh, sent, 0)

    def zh_first(left, right, pick, start, lanes, shape):
        def product(a, b):
            return columns(*pick(a, b), start * HEAD, (start + lanes) * HEAD, (2,) + shape).swapaxes(0, 2)

        return Reduction(Step(product, left, right), over_zh, over_x)

    def slabs(parts):
        parts = [part.astype(BF16).reshape(MEMBERS, -1, part.shape[-1]) for part in parts]
        return exchange(jnp.concatenate(parts, axis=2), CORE, ZL, Y)

    hidden_partial = Step(lambda a: product_sums(core, a[1], a[2], True), forward)
    hidden_sums = Step(collect, hidden_partial)
    down_pick, down_shape = lambda a, b: (a[0], b), (1, 2)
    grad_down = [
        x_first(forward, all_cotangent, down_pick, 0, 12, down_shape),
        zh_first(forward, all_cotangent, down_pick, 12, 4, down_shape),
    ]
    down_out = Step(
        lambda *parts: jnp.concatenate([part[0] for part in parts], axis=1), *[part.total for part in grad_down]
    )
    up_pick, up_shape = lambda a, b: (a, b[1]), (2, 2)
    grad_up = [x_first(normal_two, forward, up_pick, start, 4, up_shape) for start in (0, 4)]
    up_slabs = Step(lambda *parts: slabs(parts), *[part.total for part in grad_up])
    up_out = Step(lambda a: place_columns([a], up_weight, second_column, up_columns), up_slabs)
    layer_partial = Step(lambda a, down: product_sums(core, a[0], down), forward, down)
    layer_sums = Step(collect, layer_partial)
    layer_rows = Step(
        lambda a, middle: (middle[0] + jnp.sum(a.astype(F32), axis=0)).astype(BF16), layer_sums, middle
    )
    layer_output = Step(regroup, layer_rows)
    grad_middle = Step(
        lambda a, middle, cot, gains: grad_middle_rows(a, middle[0], cot, gains[1:]),
        hidden_sums,
        middle,
        own_cotangent,
        gains,
    )
    grad_branch = Step(lambda a: gather(a[1], CORE, ZL, Y), grad_middle)
    grad_attended = Step(lambda a, output: dot_transposed(a, output).astype(BF16), grad_branch, output)
    grad_mixed = Step(
        lambda ends, a, grad, cosine, sine: attention_backward_heads(ends, a[0], a[1], a[2], grad, cosine, sine),
        ends,
        attention,
        grad_attended,
        cosine,
        sine,
    )
    output_term = Reduction(
        Step(
            lambda a, b: contract_rows(a[3], b).astype(BF16).reshape(2, 2, -1, width).swapaxes(0, 1)[:, None],
            attention,
            grad_branch,
        ),
        over_x,
        over_zh,
    )
    output_grad = Step(
        lambda a: lax.ppermute(a[0].astype(BF16), AXES, turn_pairs()).astype(F32), output_term.total
    )
    mixed_partial = Step(lambda a, b: product_sums(core, a, b[4], True), grad_mixed, attention)
    mixed_sums = Step(collect, mixed_partial)
    token_rows = Step(
        lambda a, inputs, middle, gains: token_grad_rows(a, inputs, middle[0], gains[:1]),
        mixed_sums,
        inputs,
        grad_middle,
        gains,
    )
    token_grad = Step(regroup, token_rows)
    grad_triple = [x_first(normal, grad_mixed, lambda a, b: (a, b), 0, 6, (2, 2))]
    triple_slabs = Step(lambda *parts: slabs(parts), *[part.total for part in grad_triple])
    triple_out = Step(lambda a: place_columns([a], triple_weight, first_column, triple_columns), triple_slabs)

    windows = [
        (
            [
                triple_own, triple_half[0], triple_half[1], gains_own, inputs, own_cotangent, down_x, turned,
                ends, down_part[0], down_part[1], down_part[2], down_part[3], up_dealt,
            ],
            [],
        ),
        (
            [all_inputs, triple_zh[0], triple_zh[1], triple_x, gains_pair, gains, cosine, sine],
            [down_part[0], turned],
        ),
        (
            [triple_xz[0], triple_xz[1], turned_zh, turned_pair, down_zh[0], normal],
            [
                cosine, down_part[1], down_part[2], ends, sine, triple_own, triple_x, triple_zh[0],
                triple_zh[1], up_dealt,
            ],
        ),
        (
            [up_own, up_half[0], up_half[1], turned_x, output, down_zh[1], down_zh[2], down_xz[0], attention],
            [down_part[3]],
        ),
        (
            [attended_partial, attended_sums, up_zh[0], up_x, down_zh[3], down_xz[1], down_xz[2]],
            [down_own, down_x, down_xz[0], down_zh[0], down_zh[1], down_zh[2], gains, inputs, up_half[1]],
        ),
        (
            [middle, normal_two, up_zh[1], up_xz[0], down_xz[3], up_xz[1], down, grad_activation],
            [up_own, up_x, up_zh[0]],
        ),
        (
            [forward],
            [all_cotangent],
        ),
        (
            [hidden_partial, grad_down[0].sent],
            [all_cotangent, forward, normal_two],
        ),
        (
            [
                hidden_sums, grad_down[1].kept, grad_down[0].came, grad_down[1].came, grad_up[0].sent,
                grad_down[0].kept,
            ],
            [down, forward, gains, middle, normal_two, own_cotangent],
        ),
        (
            [
                grad_middle, grad_branch, grad_up[0].came, grad_down[1].far, grad_down[0].far, grad_up[1].sent,
                grad_up[1].kept, layer_partial, grad_up[0].kept,
            ],
            [attention, cosine, ends, normal, output, sine],
        ),
        (
            [
                layer_sums, grad_up[1].came, grad_up[0].far, grad_attended, grad_mixed, mixed_partial,
                grad_triple[0].sent,
            ],
            [attention, grad_branch, normal],
        ),
        (
            [
                mixed_sums, grad_triple[0].came, grad_up[1].far, layer_output, grad_triple[0].kept,
                output_term.kept,
            ],
            [gains, grad_middle, inputs],
        ),
        (
            [grad_triple[0].far, output_term.came, token_rows, up_slabs],
            [],
        ),
    ]
    for made, held in windows:
        values = together(*[step.get() for step in made + held])
        for step, value in zip(made + held, values):
            step.put(value)
    return (
        layer_output.get(),
        token_grad.get(),
        triple_out.get()[0],
        output_grad.get(),
        up_out.get()[0],
        down_out.get(),
        triple_out.get()[1][:, 0],
        up_out.get()[1][:, 0],
    )


def solution(mesh):
    grouped = mesh.shape["dp"] * 2 == mesh.shape["fsdp"] == MEMBERS
    rows = P(AXES, None)
    return jax.shard_map(
        grouped_body if grouped else whole_rows_body,
        mesh=mesh,
        in_specs=(rows,) * 5 + (P(AXES),) * 2 + (rows, P("dp", None), P("dp", None, None), P("dp", None, None)),
        out_specs=(rows,) * 6 + (P(AXES),) * 2,
        check_vma=False,
    )
```

profile of v0, /device:TPU:27, one launch (start us, length us, event | category | flops | bytes accessed | tf_op | source)
XLA Modules:
  0.0 569.3 jit_solution(9488108265546466463)
XLA Ops:
  9.5 4.6 all-to-all-start
  15.0 5.4 collective-permute-start
  20.4 5.4 collective-permute-start.1
  25.7 4.0 collective-permute-start.3
  39.6 6.3 %collective-permute-done.3 = bf16[64,2048]{1,0:T(8,128)(2,1)S(1)} collective-permute-done((bf16[64,2048]{1,0:T(8,128)(2,1)}, bf16[64,2048]{1,0:T(8,128)(2,1)S(1)}, u32[]{:S(2)}, u32[]{:S(2)}) %collective-permute-start.3) | collective-permute-done | bytes 262176 | tf_op jit(solution)/shard_map/ppermute | solution.py:990
  55.2 9.1 %collective-permute-done.9 = bf16[2,8,128]{2,1,0:T(8,128)(2,1)} collective-permute-done((bf16[2,8,128]{2,1,0:T(8,128)(2,1)}, bf16[2,8,128]{2,1,0:T(8,128)(2,1)}, u32[]{:S(2)}, u32[]{:S(2)}) %collective-permute-start.9) | collective-permute-done | bytes 4128 | tf_op jit(solution)/shard_map/ppermute | solution.py:426
  68.4 4.7 collective-permute-done.5.rest_1_
  73.1 13.2 %collective-permute-done.6.rest_2_ = bf16[256,768]{1,0:T(8,128)(2,1)} collective-permute-done((bf16[256,768]{1,0:T(8,128)(2,1)}, bf16[256,768]{1,0:T(8,128)(2,1)}, u32[]{:S(2)}, u32[]{:S(2)}) %collective-permute-start.6) | collective-permute-done | bytes 393248 | tf_op jit(solution)/shard_map/ppermute | solution.py:426
  86.3 5.5 all-gather.5.cloned.1.call-done.values_ref
  96.9 12.0 %shard_map.172.normal_ref = bf16[1024,2048]{1,0:T(8,128)(2,1)} custom-call(bf16[1024,2048]{1,0:T(8,128)(2,1)} %all-gather.5.cloned.1.call-done.values_ref, f32[1,2048]{1,0:T(1,128)} %slice.110.gain_ref), custom_call_target="tpu_custom_call" | custom-call | tf_op jit(solution)/shard_map/pallas_call | solution.py:776
  111.8 3.7 collective-permute-done.13.rest_2_
  117.0 3.8 all-to-all-start.1
  129.1 14.0 %shard_map.173 = (bf16[1024,256]{1,0:T(8,128)(2,1)S(1)}, bf16[1024,256]{1,0:T(8,128)(2,1)S(1)}, bf16[1024,256]{1,0:T(8,128)(2,1)S(1)}, bf16[1024,256]{1,0:T(8,128)(2,1)S(1)}, bf16[2048,768]{1,0:T(8,128)(2,1)}) custom-call(s32[2]{0:T(128)S(1)} %pad_add_fusion.1.ends_ref, s32[8]{0:T(128)S(1)} %stack.163.places_ref, bf16[1024,2048]{1,0:T(8,128)(2,1)} %shard_map.172.normal_ref, ...), custom_call_target="tpu_custom_call" | custom-call | tf_op jit(solution)/shard_map/pallas_call | solution.py:696
  145.3 6.8 %all-to-all-done.1 = bf16[8,64,1024]{2,1,0:T(8,128)(2,1)S(1)} async-done(((bf16[8,64,1024]{2,1,0:T(8,128)(2,1)}), bf16[8,64,1024]{2,1,0:T(8,128)(2,1)S(1)}, u32[]{:S(2)}, u32[]{:S(2)}) %all-to-all-start.1) | async-done | bytes 1048608 | tf_op jit(solution)/shard_map/all_to_all | solution.py:437
  157.1 3.8 collective-permute-done.18.rest_0_
  163.8 9.9 %all-to-all-start.2 = ((bf16[4,128,2048]{2,1,0:T(8,128)(2,1)}), bf16[4,128,2048]{2,1,0:T(8,128)(2,1)}, u32[]{:S(2)}, u32[]{:S(2)}) async-start(bf16[4,128,2048]{2,1,0:T(8,128)(2,1)} %bitcast.180), calls=%async_computation.2 | async-start | bytes 4194304 | tf_op jit(solution)/shard_map/all_to_all | solution.py:437
  178.8 34.4 %collective-permute-done.21.rest_5_ = bf16[64,2048]{1,0:T(8,128)(2,1)S(1)} collective-permute-done((bf16[64,2048]{1,0:T(8,128)(2,1)}, bf16[64,2048]{1,0:T(8,128)(2,1)S(1)}, u32[]{:S(2)}, u32[]{:S(2)}) %collective-permute-start.21) | collective-permute-done | bytes 262176 | tf_op jit(solution)/shard_map/ppermute | solution.py:426
  223.8 4.9 collective-permute-done.26.rest_9_
  235.9 9.6 %collective-permute-done.24.rest_2_ = bf16[256,1024]{1,0:T(8,128)(2,1)} collective-permute-done((bf16[256,1024]{1,0:T(8,128)(2,1)}, bf16[256,1024]{1,0:T(8,128)(2,1)}, u32[]{:S(2)}, u32[]{:S(2)}) %collective-permute-start.24) | collective-permute-done | bytes 524320 | tf_op jit(solution)/shard_map/ppermute | solution.py:426
  246.0 10.1 %fusion.81.grad_activation_ref = f32[1024,1024]{1,0:T(8,128)} fusion(bf16[1024,2048]{1,0:T(8,128)(2,1)} %all-gather.9.cloned.1.call-done, bf16[1024,2048]{1,0:T(8,128)(2,1)} %copy-done), kind=kOutput, calls=%fused_computation.112 | convolution fusion | flops 4294967296 | bytes 12582912 | tf_op jit(solution)/shard_map/dot_general | solution.py:888
  261.2 11.8 %shard_map.178 = (bf16[1024,1024]{1,0:T(8,128)(2,1)}, bf16[1024,1024]{1,0:T(8,128)(2,1)}, bf16[2048,1024]{1,0:T(8,128)(2,1)}) custom-call(s32[8]{0:T(128)S(1)} %stack.163.places_ref, bf16[1024,2048]{1,0:T(8,128)(2,1)} %all-gather.7.cloned.1.call-done.normal_ref, f32[1024,1024]{1,0:T(8,128)} %fusion.81.grad_activation_ref, bf16[512,1024]{1,0:T(8,128)(2,1)S(1)} %bitcast.175, ...), custom_call_target="tpu_custom_call" | custom-call | tf_op jit(solution)/shard_map/pallas_call | solution.py:867
  276.9 3.9 shard_map.179
  281.1 5.0 fusion.4
  286.1 5.4 shard_map.180
  291.5 4.4 all-to-all-start.3
  303.1 3.1 fusion.7
  306.1 23.9 %collective-permute-done.30 = bf16[1,2,256,512]{3,2,1,0:T(8,128)(2,1)} collective-permute-done((bf16[1,2,256,512]{3,2,1,0:T(8,128)(2,1)S(1)}, bf16[1,2,256,512]{3,2,1,0:T(8,128)(2,1)}, u32[]{:S(2)}, u32[]{:S(2)}) %collective-permute-start.30) | collective-permute-done | bytes 524320 | tf_op jit(solution)/shard_map/ppermute | solution.py:426
  332.9 3.4 shard_map.181
  338.5 4.0 shard_map.182
  350.4 4.0 fusion.37
  359.0 5.4 shard_map.183
  364.4 13.5 %collective-permute-done.32 = bf16[1,256,512]{2,1,0:T(8,128)(2,1)S(1)} collective-permute-done((bf16[1,256,512]{2,1,0:T(8,128)(2,1)S(1)}, bf16[1,256,512]{2,1,0:T(8,128)(2,1)S(1)}, u32[]{:S(2)}, u32[]{:S(2)}) %collective-permute-start.32) | collective-permute-done | bytes 262176 | tf_op jit(solution)/shard_map/ppermute | solution.py:426
  377.9 3.9 collective-permute-done.33
  382.7 6.0 %all-to-all-start.4 = ((bf16[4,128,2048]{2,1,0:T(8,128)(2,1)}), bf16[4,128,2048]{2,1,0:T(8,128)(2,1)}, u32[]{:S(2)}, u32[]{:S(2)}) async-start(bf16[4,128,2048]{2,1,0:T(8,128)(2,1)} %bitcast.61), calls=%async_computation.4 | async-start | bytes 4194304 | tf_op jit(solution)/shard_map/all_to_all | solution.py:437
  388.8 3.6 convolution_convert_fusion.2.g_ref
  392.5 7.8 %shard_map.184.left_ref = bf16[1024,768]{1,0:T(8,128)(2,1)S(1)} custom-call(s32[2]{0:T(128)S(1)} %pad_add_fusion.1.ends_ref, bf16[1024,256]{1,0:T(8,128)(2,1)S(1)} %copy-done.30, bf16[1024,256]{1,0:T(8,128)(2,1)S(1)} %copy-done.32, bf16[1024,256]{1,0:T(8,128)(2,1)S(1)} %copy-done.34, bf16[1024,256]{1,0:T(8,128)(2,1)S(1)} %convolution_convert_fusion.2.g_ref, ...), custom_call_target="tpu_custom_call" | custom-call | tf_op jit(solution)/shard_map/pallas_call | solution.py:743
  411.4 19.2 %collective-permute-done.36 = bf16[2,256,512]{2,1,0:T(8,128)(2,1)} collective-permute-done((bf16[2,256,512]{2,1,0:T(8,128)(2,1)S(1)}, bf16[2,256,512]{2,1,0:T(8,128)(2,1)}, u32[]{:S(2)}, u32[]{:S(2)}) %collective-permute-start.36) | collective-permute-done | bytes 524320 | tf_op jit(solution)/shard_map/ppermute | solution.py:426
  430.6 4.7 all-to-all-start.5
  441.4 4.7 collective-permute-start.39
  453.7 25.9 %collective-permute-done.39 = bf16[2,256,512]{2,1,0:T(8,128)(2,1)} collective-permute-done((bf16[2,256,512]{2,1,0:T(8,128)(2,1)S(1)}, bf16[2,256,512]{2,1,0:T(8,128)(2,1)}, u32[]{:S(2)}, u32[]{:S(2)}) %collective-permute-start.39) | collective-permute-done | bytes 524320 | tf_op jit(solution)/shard_map/ppermute | solution.py:426
  482.2 4.0 all-to-all-start.6
  490.0 3.2 shard_map.187
  493.2 8.9 %collective-permute-done.42 = bf16[1,2,64,2048]{3,2,1,0:T(8,128)(2,1)S(1)} collective-permute-done((bf16[1,2,64,2048]{3,2,1,0:T(8,128)(2,1)}, bf16[1,2,64,2048]{3,2,1,0:T(8,128)(2,1)S(1)}, u32[]{:S(2)}, u32[]{:S(2)}) %collective-permute-start.42) | collective-permute-done | bytes 524320 | tf_op jit(solution)/shard_map/ppermute | solution.py:426
  502.1 22.3 %collective-permute-done.41 = bf16[2,256,768]{2,1,0:T(8,128)(2,1)} collective-permute-done((bf16[2,256,768]{2,1,0:T(8,128)(2,1)S(1)}, bf16[2,256,768]{2,1,0:T(8,128)(2,1)}, u32[]{:S(2)}, u32[]{:S(2)}) %collective-permute-start.41) | collective-permute-done | bytes 786464 | tf_op jit(solution)/shard_map/ppermute | solution.py:426
  527.5 5.0 all-to-all-start.7
  535.4 5.4 collective-permute-start.43
  541.8 3.5 collective-permute-start.45
  549.1 6.8 %collective-permute-done.45 = bf16[64,2048]{1,0:T(8,128)(2,1)} collective-permute-done((bf16[64,2048]{1,0:T(8,128)(2,1)S(1)}, bf16[64,2048]{1,0:T(8,128)(2,1)}, u32[]{:S(2)}, u32[]{:S(2)}) %collective-permute-start.45) | collective-permute-done | bytes 262176 | tf_op jit(solution)/shard_map/ppermute | solution.py:1122
  (323 shorter events, 159.1 us)
Async XLA Ops:
  9.5 26.5 %all-to-all-start = ((bf16[8,80,768]{2,1,0:T(8,128)(2,1)}), bf16[8,80,768]{2,1,0:T(8,128)(2,1)S(1)}, u32[]{:S(2)}, u32[]{:S(2)}) async-start(bf16[8,80,768]{2,1,0:T(8,128)(2,1)} %shard_map.170), calls=%async_computation | async-start | bytes 1966080 | tf_op jit(solution)/shard_map/all_to_all | solution.py:437
  14.1 77.7 %all-gather.5.cloned.1.call-start = ((), (), s32[]{:S(2)}) async-start(), calls=%async_computation.8 | async-start | bytes 4718592 | tf_op jit(solution)/shard_map/all_gather | solution.py:465
  14.4 18.7 %collective-permute-start.4 = (s32[18]{0:T(128)S(1)}, s32[18]{0:T(128)S(1)}, u32[]{:S(2)}, u32[]{:S(2)}) collective-permute-start(s32[18]{0:T(128)S(1)} %pad_add_fusion), channel_id=1, source_target_pairs={{0,8},{1,9},{2,10},{3,11},{4,12},{5,13},{6,14},{7,15},{8,0},{9,1},... | collective-permute-start | bytes 224 | tf_op jit(solution)/shard_map/ppermute | solution.py:426
  14.7 31.1 %collective-permute-start.2 = (bf16[256,2048]{1,0:T(8,128)(2,1)S(1)}, bf16[256,2048]{1,0:T(8,128)(2,1)S(1)}, u32[]{:S(2)}, u32[]{:S(2)}) collective-permute-start(bf16[256,2048]{1,0:T(8,128)(2,1)S(1)} %copy-done.17), channel_id=1, source_target_pairs={{0,16},{1,17},{2,18},{3,19},{4,20},{5,21},{6,22},{7,23},{8,24},{9,... | collective-permute-start | bytes 3145736 | tf_op jit(solution)/shard_map/ppermute | solution.py:426
  15.0 30.9 %collective-permute-start = (bf16[128,2048]{1,0:T(8,128)(2,1)}, bf16[128,2048]{1,0:T(8,128)(2,1)}, u32[]{:S(2)}, u32[]{:S(2)}) collective-permute-start(bf16[128,2048]{1,0:T(8,128)(2,1)} %param.11), channel_id=1, source_target_pairs={{0,0},{1,1},{2,2},{3,3},{4,8},{5,9},{6,10},{7,11},{8,4},{9,5},{10,... | collective-permute-start | bytes 1572872 | tf_op jit(solution)/shard_map/ppermute | solution.py:457
  20.4 25.5 %collective-permute-start.1 = (bf16[128,2048]{1,0:T(8,128)(2,1)}, bf16[128,2048]{1,0:T(8,128)(2,1)}, u32[]{:S(2)}, u32[]{:S(2)}) collective-permute-start(bf16[128,2048]{1,0:T(8,128)(2,1)} %param.18), channel_id=1, source_target_pairs={{0,0},{1,1},{2,2},{3,3},{4,8},{5,9},{6,10},{7,11},{8,4},{9,5},{10,... | collective-permute-start | bytes 1572872 | tf_op jit(solution)/shard_map/ppermute | solution.py:457
  25.7 20.1 %collective-permute-start.3 = (bf16[64,2048]{1,0:T(8,128)(2,1)}, bf16[64,2048]{1,0:T(8,128)(2,1)S(1)}, u32[]{:S(2)}, u32[]{:S(2)}) collective-permute-start(bf16[64,2048]{1,0:T(8,128)(2,1)} %param.13), channel_id=1, source_target_pairs={{0,0},{1,16},{2,2},{3,18},{4,4},{5,20},{6,6},{7,22},{8,8},{9,24},{... | collective-permute-start | bytes 786440 | tf_op jit(solution)/shard_map/ppermute | solution.py:990
  45.9 40.4 %collective-permute-start.7 = (bf16[512,768]{1,0:T(8,128)(2,1)S(1)}, bf16[512,768]{1,0:T(8,128)(2,1)}, u32[]{:S(2)}, u32[]{:S(2)}) collective-permute-start(bf16[512,768]{1,0:T(8,128)(2,1)S(1)} %bitcast.181), channel_id=1, source_target_pairs={{0,16},{1,17},{2,18},{3,19},{4,20},{5,21},{6,22},{7,23},{8,24},{9,... | collective-permute-start | bytes 2359304 | tf_op jit(solution)/shard_map/ppermute | solution.py:426
  48.7 24.4 %collective-permute-start.5 = (bf16[256,768]{1,0:T(8,128)(2,1)}, bf16[256,768]{1,0:T(8,128)(2,1)S(1)}, u32[]{:S(2)}, u32[]{:S(2)}) collective-permute-start(bf16[256,768]{1,0:T(8,128)(2,1)} %bitcast.208), channel_id=1, source_target_pairs={{0,4},{1,5},{2,6},{3,7},{4,0},{5,1},{6,2},{7,3},{8,12},{9,13},{10,... | collective-permute-start | bytes 1179656 | tf_op jit(solution)/shard_map/ppermute | solution.py:426
  51.0 35.3 %collective-permute-start.6 = (bf16[256,768]{1,0:T(8,128)(2,1)}, bf16[256,768]{1,0:T(8,128)(2,1)}, u32[]{:S(2)}, u32[]{:S(2)}) collective-permute-start(bf16[256,768]{1,0:T(8,128)(2,1)} %bitcast.207), channel_id=1, source_target_pairs={{0,4},{1,5},{2,6},{3,7},{4,0},{5,1},{6,2},{7,3},{8,12},{9,13},{10,... | collective-permute-start | bytes 1179656 | tf_op jit(solution)/shard_map/ppermute | solution.py:426
  91.8 18.1 %collective-permute-start.12 = (bf16[64,2048]{1,0:T(8,128)(2,1)S(1)}, bf16[64,2048]{1,0:T(8,128)(2,1)}, u32[]{:S(2)}, u32[]{:S(2)}) collective-permute-start(bf16[64,2048]{1,0:T(8,128)(2,1)S(1)} %copy-done.65), channel_id=1, source_target_pairs={{0,4},{1,5},{2,6},{3,7},{4,0},{5,1},{6,2},{7,3},{8,12},{9,13},{10,... | collective-permute-start | bytes 786440 | tf_op jit(solution)/shard_map/ppermute | solution.py:426
  91.8 23.8 %collective-permute-start.10 = (bf16[256,768]{1,0:T(8,128)(2,1)S(1)}, bf16[256,768]{1,0:T(8,128)(2,1)S(1)}, u32[]{:S(2)}, u32[]{:S(2)}) collective-permute-start(bf16[256,768]{1,0:T(8,128)(2,1)S(1)} %collective-permute-done.5.rest_1_), channel_id=1, source_target_pairs={{0,16},{1,17},{2,18},{3,19},{4,20},{5,21},{6,22},{7,23},{8,24},{9,... | collective-permute-start | bytes 1179656 | tf_op jit(solution)/shard_map/ppermute | solution.py:426
  92.0 24.3 %collective-permute-start.11 = (bf16[256,768]{1,0:T(8,128)(2,1)}, bf16[256,768]{1,0:T(8,128)(2,1)S(1)}, u32[]{:S(2)}, u32[]{:S(2)}) collective-permute-start(bf16[256,768]{1,0:T(8,128)(2,1)} %collective-permute-done.6.rest_2_), channel_id=1, source_target_pairs={{0,16},{1,17},{2,18},{3,19},{4,20},{5,21},{6,22},{7,23},{8,24},{9,... | collective-permute-start | bytes 1179656 | tf_op jit(solution)/shard_map/ppermute | solution.py:426
  93.2 22.3 %collective-permute-start.13 = (bf16[64,2048]{1,0:T(8,128)(2,1)}, bf16[64,2048]{1,0:T(8,128)(2,1)}, u32[]{:S(2)}, u32[]{:S(2)}) collective-permute-start(bf16[64,2048]{1,0:T(8,128)(2,1)} %get-tuple-element.174), channel_id=1, source_target_pairs={{0,4},{1,5},{2,6},{3,7},{4,0},{5,1},{6,2},{7,3},{8,12},{9,13},{10,... | collective-permute-start | bytes 786440 | tf_op jit(solution)/shard_map/ppermute | solution.py:426
  117.0 35.1 %all-to-all-start.1 = ((bf16[8,64,1024]{2,1,0:T(8,128)(2,1)}), bf16[8,64,1024]{2,1,0:T(8,128)(2,1)S(1)}, u32[]{:S(2)}, u32[]{:S(2)}) async-start(bf16[8,64,1024]{2,1,0:T(8,128)(2,1)} %shard_map.171), calls=%async_computation.1 | async-start | bytes 2097152 | tf_op jit(solution)/shard_map/all_to_all | solution.py:437
  120.8 125.2 %all-gather.9.cloned.1.call-start = ((), (), s32[]{:S(2)}) async-start(), calls=%async_computation.10 | async-start | bytes 4718592 | tf_op jit(solution)/shard_map/all_gather | solution.py:465
  121.5 21.6 %collective-permute-start.14 = (bf16[2,64,2048]{2,1,0:T(8,128)(2,1)}, bf16[2,64,2048]{2,1,0:T(8,128)(2,1)}, u32[]{:S(2)}, u32[]{:S(2)}) collective-permute-start(bf16[2,64,2048]{2,1,0:T(8,128)(2,1)} %maximum_select_fusion.1), channel_id=1, source_target_pairs={{0,16},{1,17},{2,18},{3,19},{4,20},{5,21},{6,22},{7,23},{8,24},{9,... | collective-permute-start | bytes 1572872 | tf_op jit(solution)/shard_map/ppermute | solution.py:426
  122.7 30.5 %collective-permute-start.15 = (bf16[64,2048]{1,0:T(8,128)(2,1)}, bf16[64,2048]{1,0:T(8,128)(2,1)}, u32[]{:S(2)}, u32[]{:S(2)}) collective-permute-start(bf16[64,2048]{1,0:T(8,128)(2,1)} %get-tuple-element.186), channel_id=1, source_target_pairs={{0,4},{1,5},{2,6},{3,7},{4,0},{5,1},{6,2},{7,3},{8,12},{9,13},{10,... | collective-permute-start | bytes 786440 | tf_op jit(solution)/shard_map/ppermute | solution.py:426
  124.7 29.1 %collective-permute-start.16 = (bf16[64,2048]{1,0:T(8,128)(2,1)}, bf16[64,2048]{1,0:T(8,128)(2,1)}, u32[]{:S(2)}, u32[]{:S(2)}) collective-permute-start(bf16[64,2048]{1,0:T(8,128)(2,1)} %get-tuple-element.187), channel_id=1, source_target_pairs={{0,4},{1,5},{2,6},{3,7},{4,0},{5,1},{6,2},{7,3},{8,12},{9,13},{10,... | collective-permute-start | bytes 786440 | tf_op jit(solution)/shard_map/ppermute | solution.py:426
  125.1 28.8 %collective-permute-start.17 = (bf16[64,2048]{1,0:T(8,128)(2,1)}, bf16[64,2048]{1,0:T(8,128)(2,1)}, u32[]{:S(2)}, u32[]{:S(2)}) collective-permute-start(bf16[64,2048]{1,0:T(8,128)(2,1)} %collective-permute-done.13.rest_2_), channel_id=1, source_target_pairs={{0,16},{1,17},{2,18},{3,19},{4,20},{5,21},{6,22},{7,23},{8,24},{9,... | collective-permute-start | bytes 786440 | tf_op jit(solution)/shard_map/ppermute | solution.py:426
  163.8 51.8 %all-to-all-start.2 = ((bf16[4,128,2048]{2,1,0:T(8,128)(2,1)}), bf16[4,128,2048]{2,1,0:T(8,128)(2,1)}, u32[]{:S(2)}, u32[]{:S(2)}) async-start(bf16[4,128,2048]{2,1,0:T(8,128)(2,1)} %bitcast.180), calls=%async_computation.2 | async-start | bytes 4194304 | tf_op jit(solution)/shard_map/all_to_all | solution.py:437
  173.8 87.5 %all-gather.7.cloned.1.call-start = ((), (), s32[]{:S(2)}) async-start(), calls=%async_computation.9 | async-start | bytes 4718592 | tf_op jit(solution)/shard_map/all_gather | solution.py:465
  174.2 40.4 %collective-permute-start.20 = (bf16[512,1024]{1,0:T(8,128)(2,1)S(1)}, bf16[512,1024]{1,0:T(8,128)(2,1)S(1)}, u32[]{:S(2)}, u32[]{:S(2)}) collective-permute-start(bf16[512,1024]{1,0:T(8,128)(2,1)S(1)} %bitcast.174), channel_id=1, source_target_pairs={{0,16},{1,17},{2,18},{3,19},{4,20},{5,21},{6,22},{7,23},{8,24},{9,... | collective-permute-start | bytes 3145736 | tf_op jit(solution)/shard_map/ppermute | solution.py:426
  175.0 39.7 %collective-permute-start.19 = (bf16[256,1024]{1,0:T(8,128)(2,1)}, bf16[256,1024]{1,0:T(8,128)(2,1)}, u32[]{:S(2)}, u32[]{:S(2)}) collective-permute-start(bf16[256,1024]{1,0:T(8,128)(2,1)} %bitcast.206), channel_id=1, source_target_pairs={{0,4},{1,5},{2,6},{3,7},{4,0},{5,1},{6,2},{7,3},{8,12},{9,13},{10,... | collective-permute-start | bytes 1572872 | tf_op jit(solution)/shard_map/ppermute | solution.py:426
  175.0 38.2 %collective-permute-start.21 = (bf16[64,2048]{1,0:T(8,128)(2,1)}, bf16[64,2048]{1,0:T(8,128)(2,1)S(1)}, u32[]{:S(2)}, u32[]{:S(2)}) collective-permute-start(bf16[64,2048]{1,0:T(8,128)(2,1)} %get-tuple-element.209), channel_id=1, source_target_pairs={{0,4},{1,5},{2,6},{3,7},{4,0},{5,1},{6,2},{7,3},{8,12},{9,13},{10,... | collective-permute-start | bytes 786440 | tf_op jit(solution)/shard_map/ppermute | solution.py:426
  177.3 35.9 %collective-permute-start.22 = (bf16[64,2048]{1,0:T(8,128)(2,1)}, bf16[64,2048]{1,0:T(8,128)(2,1)S(1)}, u32[]{:S(2)}, u32[]{:S(2)}) collective-permute-start(bf16[64,2048]{1,0:T(8,128)(2,1)} %collective-permute-done.15.rest_3_), channel_id=1, source_target_pairs={{0,16},{1,17},{2,18},{3,19},{4,20},{5,21},{6,22},{7,23},{8,24},{9,... | collective-permute-start | bytes 786440 | tf_op jit(solution)/shard_map/ppermute | solution.py:426
  178.1 35.8 %collective-permute-start.23 = (bf16[64,2048]{1,0:T(8,128)(2,1)}, bf16[64,2048]{1,0:T(8,128)(2,1)S(1)}, u32[]{:S(2)}, u32[]{:S(2)}) collective-permute-start(bf16[64,2048]{1,0:T(8,128)(2,1)} %collective-permute-done.16.rest_4_), channel_id=1, source_target_pairs={{0,16},{1,17},{2,18},{3,19},{4,20},{5,21},{6,22},{7,23},{8,24},{9,... | collective-permute-start | bytes 786440 | tf_op jit(solution)/shard_map/ppermute | solution.py:426
  219.1 26.5 %collective-permute-start.24 = (bf16[256,1024]{1,0:T(8,128)(2,1)}, bf16[256,1024]{1,0:T(8,128)(2,1)}, u32[]{:S(2)}, u32[]{:S(2)}) collective-permute-start(bf16[256,1024]{1,0:T(8,128)(2,1)} %bitcast.205), channel_id=1, source_target_pairs={{0,4},{1,5},{2,6},{3,7},{4,0},{5,1},{6,2},{7,3},{8,12},{9,13},{10,... | collective-permute-start | bytes 1572872 | tf_op jit(solution)/shard_map/ppermute | solution.py:426
  222.8 33.3 %collective-permute-start.25 = (bf16[256,1024]{1,0:T(8,128)(2,1)}, bf16[256,1024]{1,0:T(8,128)(2,1)}, u32[]{:S(2)}, u32[]{:S(2)}) collective-permute-start(bf16[256,1024]{1,0:T(8,128)(2,1)} %collective-permute-done.19.rest_1_), channel_id=1, source_target_pairs={{0,16},{1,17},{2,18},{3,19},{4,20},{5,21},{6,22},{7,23},{8,24},{9,... | collective-permute-start | bytes 1572872 | tf_op jit(solution)/shard_map/ppermute | solution.py:426
  291.5 40.8 %all-to-all-start.3 = ((bf16[4,128,2048]{2,1,0:T(8,128)(2,1)}), bf16[4,128,2048]{2,1,0:T(8,128)(2,1)}, u32[]{:S(2)}, u32[]{:S(2)}) async-start(bf16[4,128,2048]{2,1,0:T(8,128)(2,1)} %bitcast.48), calls=%async_computation.3 | async-start | bytes 4194304 | tf_op jit(solution)/shard_map/all_to_all | solution.py:437
  296.0 86.7 %all-gather.11.cloned.1.call-start = ((), (), s32[]{:S(2)}) async-start(), calls=%async_computation.11 | async-start | bytes 4718592 | tf_op jit(solution)/shard_map/all_gather | solution.py:465
  296.2 36.1 %collective-permute-start.29 = (bf16[1,2,256,1536]{3,2,1,0:T(8,128)(2,1)}, bf16[1,2,256,1536]{3,2,1,0:T(8,128)(2,1)}, u32[]{:S(2)}, u32[]{:S(2)}) collective-permute-start(bf16[1,2,256,1536]{3,2,1,0:T(8,128)(2,1)} %bitcast.217), channel_id=1, source_target_pairs={{0,16},{1,17},{2,18},{3,19},{4,20},{5,21},{6,22},{7,23},{8,24},{9,... | collective-permute-start | bytes 4718600 | tf_op jit(solution)/shard_map/ppermute | solution.py:426
  299.3 30.8 %collective-permute-start.30 = (bf16[1,2,256,512]{3,2,1,0:T(8,128)(2,1)S(1)}, bf16[1,2,256,512]{3,2,1,0:T(8,128)(2,1)}, u32[]{:S(2)}, u32[]{:S(2)}) collective-permute-start(bf16[1,2,256,512]{3,2,1,0:T(8,128)(2,1)S(1)} %dynamic-slice_bitcast_fusion.1), channel_id=1, source_target_pairs={{0,4},{1,5},{2,6},{3,7},{4,0},{5,1},{6,2},{7,3},{8,12},{9,13},{10,... | collective-permute-start | bytes 1572872 | tf_op jit(solution)/shard_map/ppermute | solution.py:426
  342.5 16.4 %collective-permute-start.34 = (bf16[512,2048]{1,0:T(8,128)(2,1)}, bf16[512,2048]{1,0:T(8,128)(2,1)}, u32[]{:S(2)}, u32[]{:S(2)}) collective-permute-start(bf16[512,2048]{1,0:T(8,128)(2,1)} %shard_map.182), channel_id=1, source_target_pairs={{0,8},{1,9},{2,10},{3,11},{4,12},{5,13},{6,14},{7,15},{8,0},{9,1},... | collective-permute-start | bytes 6291464 | tf_op jit(solution)/shard_map/ppermute | solution.py:426
  345.4 36.4 %collective-permute-start.33 = (bf16[1,256,1536]{2,1,0:T(8,128)(2,1)S(1)}, bf16[1,256,1536]{2,1,0:T(8,128)(2,1)S(1)}, u32[]{:S(2)}, u32[]{:S(2)}) collective-permute-start(bf16[1,256,1536]{2,1,0:T(8,128)(2,1)S(1)} %fusion.33), channel_id=1, source_target_pairs={{0,4},{1,5},{2,6},{3,7},{4,0},{5,1},{6,2},{7,3},{8,12},{9,13},{10,... | collective-permute-start | bytes 2359304 | tf_op jit(solution)/shard_map/ppermute | solution.py:426
  347.7 35.0 %collective-permute-start.31 = (bf16[2,2,256,512]{3,2,0,1:T(8,128)(2,1)S(1)}, bf16[2,2,256,512]{3,2,0,1:T(8,128)(2,1)}, u32[]{:S(2)}, u32[]{:S(2)}) collective-permute-start(bf16[2,2,256,512]{3,2,0,1:T(8,128)(2,1)S(1)} %copy.68), channel_id=1, source_target_pairs={{0,16},{1,17},{2,18},{3,19},{4,20},{5,21},{6,22},{7,23},{8,24},{9,... | collective-permute-start | bytes 3145736 | tf_op jit(solution)/shard_map/ppermute | solution.py:426
  349.1 28.8 %collective-permute-start.32 = (bf16[1,256,512]{2,1,0:T(8,128)(2,1)S(1)}, bf16[1,256,512]{2,1,0:T(8,128)(2,1)S(1)}, u32[]{:S(2)}, u32[]{:S(2)}) collective-permute-start(bf16[1,256,512]{2,1,0:T(8,128)(2,1)S(1)} %fusion.64), channel_id=1, source_target_pairs={{0,16},{1,17},{2,18},{3,19},{4,20},{5,21},{6,22},{7,23},{8,24},{9,... | collective-permute-start | bytes 786440 | tf_op jit(solution)/shard_map/ppermute | solution.py:426
  382.7 47.9 %all-to-all-start.4 = ((bf16[4,128,2048]{2,1,0:T(8,128)(2,1)}), bf16[4,128,2048]{2,1,0:T(8,128)(2,1)}, u32[]{:S(2)}, u32[]{:S(2)}) async-start(bf16[4,128,2048]{2,1,0:T(8,128)(2,1)} %bitcast.61), calls=%async_computation.4 | async-start | bytes 4194304 | tf_op jit(solution)/shard_map/all_to_all | solution.py:437
  403.6 27.0 %collective-permute-start.35 = (bf16[2,2,256,512]{3,2,0,1:T(8,128)(2,1)S(1)}, bf16[2,2,256,512]{3,2,0,1:T(8,128)(2,1)}, u32[]{:S(2)}, u32[]{:S(2)}) collective-permute-start(bf16[2,2,256,512]{3,2,0,1:T(8,128)(2,1)S(1)} %copy.69), channel_id=1, source_target_pairs={{0,16},{1,17},{2,18},{3,19},{4,20},{5,21},{6,22},{7,23},{8,24},{9,... | collective-permute-start | bytes 3145736 | tf_op jit(solution)/shard_map/ppermute | solution.py:426
  405.3 25.3 %collective-permute-start.36 = (bf16[2,256,512]{2,1,0:T(8,128)(2,1)S(1)}, bf16[2,256,512]{2,1,0:T(8,128)(2,1)}, u32[]{:S(2)}, u32[]{:S(2)}) collective-permute-start(bf16[2,256,512]{2,1,0:T(8,128)(2,1)S(1)} %fusion.51), channel_id=1, source_target_pairs={{0,4},{1,5},{2,6},{3,7},{4,0},{5,1},{6,2},{7,3},{8,12},{9,13},{10,... | collective-permute-start | bytes 1572872 | tf_op jit(solution)/shard_map/ppermute | solution.py:426
  430.6 48.9 %all-to-all-start.5 = ((bf16[4,128,2048]{2,1,0:T(8,128)(2,1)}), bf16[4,128,2048]{2,1,0:T(8,128)(2,1)}, u32[]{:S(2)}, u32[]{:S(2)}) async-start(bf16[4,128,2048]{2,1,0:T(8,128)(2,1)} %bitcast.179), calls=%async_computation.5 | async-start | bytes 4194304 | tf_op jit(solution)/shard_map/all_to_all | solution.py:437
  435.4 44.1 %collective-permute-start.38 = (bf16[2,2,256,768]{3,2,0,1:T(8,128)(2,1)S(1)}, bf16[2,2,256,768]{3,2,0,1:T(8,128)(2,1)}, u32[]{:S(2)}, u32[]{:S(2)}) collective-permute-start(bf16[2,2,256,768]{3,2,0,1:T(8,128)(2,1)S(1)} %copy.71), channel_id=1, source_target_pairs={{0,16},{1,17},{2,18},{3,19},{4,20},{5,21},{6,22},{7,23},{8,24},{9,... | collective-permute-start | bytes 4718600 | tf_op jit(solution)/shard_map/ppermute | solution.py:426
  441.4 38.2 %collective-permute-start.39 = (bf16[2,256,512]{2,1,0:T(8,128)(2,1)S(1)}, bf16[2,256,512]{2,1,0:T(8,128)(2,1)}, u32[]{:S(2)}, u32[]{:S(2)}) collective-permute-start(bf16[2,256,512]{2,1,0:T(8,128)(2,1)S(1)} %fusion.50), channel_id=1, source_target_pairs={{0,4},{1,5},{2,6},{3,7},{4,0},{5,1},{6,2},{7,3},{8,12},{9,13},{10,... | collective-permute-start | bytes 1572872 | tf_op jit(solution)/shard_map/ppermute | solution.py:426
  482.2 42.3 %all-to-all-start.6 = ((bf16[8,64,1024]{2,1,0:T(8,128)(2,1)}), bf16[8,64,1024]{2,1,0:T(8,128)(2,1)S(1)}, u32[]{:S(2)}, u32[]{:S(2)}) async-start(bf16[8,64,1024]{2,1,0:T(8,128)(2,1)} %pad_maximum_fusion.1), calls=%async_computation.6 | async-start | bytes 2097152 | tf_op jit(solution)/shard_map/all_to_all | solution.py:437
  487.7 36.7 %collective-permute-start.41 = (bf16[2,256,768]{2,1,0:T(8,128)(2,1)S(1)}, bf16[2,256,768]{2,1,0:T(8,128)(2,1)}, u32[]{:S(2)}, u32[]{:S(2)}) collective-permute-start(bf16[2,256,768]{2,1,0:T(8,128)(2,1)S(1)} %fusion.32), channel_id=1, source_target_pairs={{0,4},{1,5},{2,6},{3,7},{4,0},{5,1},{6,2},{7,3},{8,12},{9,13},{10,... | collective-permute-start | bytes 2359304 | tf_op jit(solution)/shard_map/ppermute | solution.py:426
  524.6 16.2 %collective-permute-start.44 = (bf16[1,64,2048]{2,1,0:T(8,128)(2,1)S(1)}, bf16[1,64,2048]{2,1,0:T(8,128)(2,1)S(1)}, u32[]{:S(2)}, u32[]{:S(2)}) collective-permute-start(bf16[1,64,2048]{2,1,0:T(8,128)(2,1)S(1)} %fusion.61), channel_id=1, source_target_pairs={{0,4},{1,5},{2,6},{3,7},{4,0},{5,1},{6,2},{7,3},{8,12},{9,13},{10,... | collective-permute-start | bytes 786440 | tf_op jit(solution)/shard_map/ppermute | solution.py:426
  527.5 30.1 %all-to-all-start.7 = ((bf16[8,64,768]{2,1,0:T(8,128)(2,1)}), bf16[8,64,768]{2,1,0:T(8,128)(2,1)S(1)}, u32[]{:S(2)}, u32[]{:S(2)}) async-start(bf16[8,64,768]{2,1,0:T(8,128)(2,1)} %bitcast.83), calls=%async_computation.7 | async-start | bytes 1572864 | tf_op jit(solution)/shard_map/all_to_all | solution.py:437
  535.4 22.2 %collective-permute-start.43 = (bf16[128,2048]{1,0:T(8,128)(2,1)}, bf16[128,2048]{1,0:T(8,128)(2,1)}, u32[]{:S(2)}, u32[]{:S(2)}) collective-permute-start(bf16[128,2048]{1,0:T(8,128)(2,1)} %shard_map.187), channel_id=1, source_target_pairs={{0,0},{1,1},{2,2},{3,3},{4,8},{5,9},{6,10},{7,11},{8,4},{9,5},{10,... | collective-permute-start | bytes 1572872 | tf_op jit(solution)/shard_map/ppermute | solution.py:457
  (84 other events, 728.3 us)
Sparse Core Ops, SparseCore 0:
  46.0 45.6 all-gather.4
  123.2 40.1 all-gather.8
  219.2 42.0 all-gather.6
  336.5 45.0 all-gather.10
where the time goes:
time: 581 us; the launch traced here: 569 us
  waiting for transfers between devices  236 us (41%)
  starting transfers between devices  104 us (18%)
  Pallas kernels  91.8 us (16%)
  local copies, waits for them, and re-layouts  45.1 us (8%)
  matrix products  41.5 us (7%)
  other arithmetic  34.7 us (6%)
  between operations  16.4 us (3%)
    ppermute x40, waiting for transfers between devices, swap(): return lax.ppermute(array, AXES, [(i, i ^ bits) for i in range(DEVICES)])  208 us
    all_to_all x8, starting transfers between devices, exchange(): lax.all_to_all(array, AXES, 0, 0, tiled=True, axis_index_groups=alike(*bi...  42.4 us
    ppermute x40, starting transfers between devices, swap(): return lax.ppermute(array, AXES, [(i, i ^ bits) for i in range(DEVICES)])  36 us
    unnamed x151, local copies, waits for them, and re-layouts  28.1 us
    dot_general x10, matrix products, contract_rows(): lax.dot_general(left, right, (((0,), (0,)), ((), ())), preferred_element_...  27.7 us
    pallas_call x8, Pallas kernels, row_product(): pl.pallas_call(kernel, grid_spec=pltpu.PrefetchScalarGridSpec(num_scalar_...  27.1 us
    ppermute x4, starting transfers between devices, regroup(): return lax.ppermute(array, AXES, regroup_pairs())  16.9 us
    pallas_call x1, Pallas kernels, attention_forward(): pl.pallas_call(kernel, out_shape=[jax.ShapeDtypeStruct((count, width), BF...  14 us
  transfers between devices with their start and end apart: 58, of which 24 were waited for; matrix products, arithmetic and copies ran while one was open for 16% of the time, Pallas kernels for 11%

commit v1 on v0

--- a/solution.py
+++ b/solution.py
@@ -1168,16 +1168,12 @@
         ),
         (
             [forward],
-            [all_cotangent],
-        ),
-        (
-            [hidden_partial, grad_down[0].sent],
-            [all_cotangent, forward, normal_two],
+            [all_cotangent, normal_two],
         ),
         (
             [
-                hidden_sums, grad_down[1].kept, grad_down[0].came, grad_down[1].came, grad_up[0].sent,
-                grad_down[0].kept,
+                hidden_partial, grad_down[0].sent, hidden_sums, grad_down[1].kept, grad_down[0].came,
+                grad_down[1].came, grad_up[0].sent, grad_down[0].kept,
             ],
             [down, forward, gains, middle, normal_two, own_cotangent],
         ),

time: 581 us -> 582 us (level)
    unnamed x151 -> x147, local copies, waits for them, and re-layouts: 28.1 us -> 28 us
  transfers between devices with their start and end apart: 58 -> 58, of which waited for: 24 -> 25; matrix products, arithmetic and copies ran while one was open for 16% -> 16% of each run, Pallas kernels for 11% -> 11%
where the time goes in v1:
time: 582 us; the launch traced here: 571 us
  waiting for transfers between devices  241 us (41%)
  starting transfers between devices  103 us (18%)
  Pallas kernels  89.6 us (15%)
  local copies, waits for them, and re-layouts  44.8 us (8%)
  matrix products  41.4 us (7%)
  other arithmetic  34.7 us (6%)
  between operations  16.4 us (3%)
    ppermute x40, waiting for transfers between devices, swap(): return lax.ppermute(array, AXES, [(i, i ^ bits) for i in range(DEVICES)])  212 us
    all_to_all x8, starting transfers between devices, exchange(): lax.all_to_all(array, AXES, 0, 0, tiled=True, axis_index_groups=alike(*bi...  42.1 us
    ppermute x40, starting transfers between devices, swap(): return lax.ppermute(array, AXES, [(i, i ^ bits) for i in range(DEVICES)])  35.5 us
    unnamed x147, local copies, waits for them, and re-layouts  28 us
    dot_general x10, matrix products, contract_rows(): lax.dot_general(left, right, (((0,), (0,)), ((), ())), preferred_element_...  27.6 us
    pallas_call x8, Pallas kernels, row_product(): pl.pallas_call(kernel, grid_spec=pltpu.PrefetchScalarGridSpec(num_scalar_...  24.9 us
    ppermute x4, starting transfers between devices, regroup(): return lax.ppermute(array, AXES, regroup_pairs())  16.9 us
    pallas_call x1, Pallas kernels, attention_forward(): pl.pallas_call(kernel, out_shape=[jax.ShapeDtypeStruct((count, width), BF...  13.9 us
  transfers between devices with their start and end apart: 58, of which 25 were waited for; matrix products, arithmetic and copies ran while one was open for 16% of the time, Pallas kernels for 11%

profile of v1, /device:TPU:27, one launch (start us, length us, event | category | flops | bytes accessed | tf_op | source)
XLA Modules:
  0.0 570.6 jit_solution(11099048923078940778)
XLA Ops:
  9.5 4.6 all-to-all-start
  15.0 5.4 collective-permute-start
  20.4 5.4 collective-permute-start.1
  25.7 4.0 collective-permute-start.3
  39.7 6.2 %collective-permute-done.3 = bf16[64,2048]{1,0:T(8,128)(2,1)S(1)} collective-permute-done((bf16[64,2048]{1,0:T(8,128)(2,1)}, bf16[64,2048]{1,0:T(8,128)(2,1)S(1)}, u32[]{:S(2)}, u32[]{:S(2)}) %collective-permute-start.3) | collective-permute-done | bytes 262176 | tf_op jit(solution)/shard_map/ppermute | solution.py:990
  55.2 9.1 %collective-permute-done.9 = bf16[2,8,128]{2,1,0:T(8,128)(2,1)} collective-permute-done((bf16[2,8,128]{2,1,0:T(8,128)(2,1)}, bf16[2,8,128]{2,1,0:T(8,128)(2,1)}, u32[]{:S(2)}, u32[]{:S(2)}) %collective-permute-start.9) | collective-permute-done | bytes 4128 | tf_op jit(solution)/shard_map/ppermute | solution.py:426
  68.4 4.7 collective-permute-done.5.rest_1_
  73.2 13.2 %collective-permute-done.6.rest_2_ = bf16[256,768]{1,0:T(8,128)(2,1)} collective-permute-done((bf16[256,768]{1,0:T(8,128)(2,1)}, bf16[256,768]{1,0:T(8,128)(2,1)}, u32[]{:S(2)}, u32[]{:S(2)}) %collective-permute-start.6) | collective-permute-done | bytes 393248 | tf_op jit(solution)/shard_map/ppermute | solution.py:426
  86.3 5.4 all-gather.5.cloned.1.call-done.values_ref
  96.9 12.0 %shard_map.172.normal_ref = bf16[1024,2048]{1,0:T(8,128)(2,1)} custom-call(bf16[1024,2048]{1,0:T(8,128)(2,1)} %all-gather.5.cloned.1.call-done.values_ref, f32[1,2048]{1,0:T(1,128)} %slice.108.gain_ref), custom_call_target="tpu_custom_call" | custom-call | tf_op jit(solution)/shard_map/pallas_call | solution.py:776
  111.8 3.7 collective-permute-done.13.rest_2_
  117.0 3.8 all-to-all-start.1
  129.1 13.9 %shard_map.173 = (bf16[1024,256]{1,0:T(8,128)(2,1)S(1)}, bf16[1024,256]{1,0:T(8,128)(2,1)S(1)}, bf16[1024,256]{1,0:T(8,128)(2,1)S(1)}, bf16[1024,256]{1,0:T(8,128)(2,1)S(1)}, bf16[2048,768]{1,0:T(8,128)(2,1)}) custom-call(s32[2]{0:T(128)S(1)} %pad_add_fusion.1.ends_ref, s32[8]{0:T(128)S(1)} %stack.163.places_ref, bf16[1024,2048]{1,0:T(8,128)(2,1)} %shard_map.172.normal_ref, ...), custom_call_target="tpu_custom_call" | custom-call | tf_op jit(solution)/shard_map/pallas_call | solution.py:696
  145.3 6.8 %all-to-all-done.1 = bf16[8,64,1024]{2,1,0:T(8,128)(2,1)S(1)} async-done(((bf16[8,64,1024]{2,1,0:T(8,128)(2,1)}), bf16[8,64,1024]{2,1,0:T(8,128)(2,1)S(1)}, u32[]{:S(2)}, u32[]{:S(2)}) %all-to-all-start.1) | async-done | bytes 1048608 | tf_op jit(solution)/shard_map/all_to_all | solution.py:437
  157.1 3.8 collective-permute-done.18.rest_0_
  163.8 9.9 %all-to-all-start.2 = ((bf16[4,128,2048]{2,1,0:T(8,128)(2,1)}), bf16[4,128,2048]{2,1,0:T(8,128)(2,1)}, u32[]{:S(2)}, u32[]{:S(2)}) async-start(bf16[4,128,2048]{2,1,0:T(8,128)(2,1)} %bitcast.180), calls=%async_computation.2 | async-start | bytes 4194304 | tf_op jit(solution)/shard_map/all_to_all | solution.py:437
  178.8 34.4 %collective-permute-done.21.rest_5_ = bf16[64,2048]{1,0:T(8,128)(2,1)S(1)} collective-permute-done((bf16[64,2048]{1,0:T(8,128)(2,1)}, bf16[64,2048]{1,0:T(8,128)(2,1)S(1)}, u32[]{:S(2)}, u32[]{:S(2)}) %collective-permute-start.21) | collective-permute-done | bytes 262176 | tf_op jit(solution)/shard_map/ppermute | solution.py:426
  223.7 4.9 collective-permute-done.26.rest_9_
  235.9 9.6 %collective-permute-done.24.rest_2_ = bf16[256,1024]{1,0:T(8,128)(2,1)} collective-permute-done((bf16[256,1024]{1,0:T(8,128)(2,1)}, bf16[256,1024]{1,0:T(8,128)(2,1)}, u32[]{:S(2)}, u32[]{:S(2)}) %collective-permute-start.24) | collective-permute-done | bytes 524320 | tf_op jit(solution)/shard_map/ppermute | solution.py:426
  246.0 10.2 %fusion.73.grad_activation_ref = f32[1024,1024]{1,0:T(8,128)} fusion(bf16[1024,2048]{1,0:T(8,128)(2,1)} %all-gather.9.cloned.1.call-done, bf16[1024,2048]{1,0:T(8,128)(2,1)} %copy-done), kind=kOutput, calls=%fused_computation.110 | convolution fusion | flops 4294967296 | bytes 12582912 | tf_op jit(solution)/shard_map/dot_general | solution.py:888
  261.2 11.8 %shard_map.178 = (bf16[1024,1024]{1,0:T(8,128)(2,1)}, bf16[1024,1024]{1,0:T(8,128)(2,1)}, bf16[2048,1024]{1,0:T(8,128)(2,1)}) custom-call(s32[8]{0:T(128)S(1)} %stack.163.places_ref, bf16[1024,2048]{1,0:T(8,128)(2,1)} %all-gather.7.cloned.1.call-done.normal_ref, f32[1024,1024]{1,0:T(8,128)} %fusion.73.grad_activation_ref, bf16[512,1024]{1,0:T(8,128)(2,1)S(1)} %bitcast.175, ...), custom_call_target="tpu_custom_call" | custom-call | tf_op jit(solution)/shard_map/pallas_call | solution.py:867
  280.3 3.9 collective-permute-done.28.rest_0_
  284.2 4.1 shard_map.180
  288.2 4.6 all-to-all-start.3
  293.1 4.9 convolution_convert_fusion.1
  307.8 19.0 %collective-permute-done.30 = bf16[1,2,256,512]{3,2,1,0:T(8,128)(2,1)} collective-permute-done((bf16[1,2,256,512]{3,2,1,0:T(8,128)(2,1)S(1)}, bf16[1,2,256,512]{3,2,1,0:T(8,128)(2,1)}, u32[]{:S(2)}, u32[]{:S(2)}) %collective-permute-start.30) | collective-permute-done | bytes 524320 | tf_op jit(solution)/shard_map/ppermute | solution.py:426
  326.9 7.1 %collective-permute-done.29 = bf16[1,2,256,1536]{3,2,1,0:T(8,128)(2,1)} collective-permute-done((bf16[1,2,256,1536]{3,2,1,0:T(8,128)(2,1)}, bf16[1,2,256,1536]{3,2,1,0:T(8,128)(2,1)}, u32[]{:S(2)}, u32[]{:S(2)}) %collective-permute-start.29) | collective-permute-done | bytes 1572896 | tf_op jit(solution)/shard_map/ppermute | solution.py:426
  334.5 3.4 shard_map.181
  340.2 4.0 shard_map.182
  351.2 4.0 fusion.29
  359.7 5.4 shard_map.183
  365.1 13.9 %collective-permute-done.32 = bf16[1,256,512]{2,1,0:T(8,128)(2,1)S(1)} collective-permute-done((bf16[1,256,512]{2,1,0:T(8,128)(2,1)S(1)}, bf16[1,256,512]{2,1,0:T(8,128)(2,1)S(1)}, u32[]{:S(2)}, u32[]{:S(2)}) %collective-permute-start.32) | collective-permute-done | bytes 262176 | tf_op jit(solution)/shard_map/ppermute | solution.py:426
  379.1 4.4 collective-permute-done.33
  384.4 5.6 all-to-all-start.4
  390.1 3.6 convolution_convert_fusion.4.g_ref
  393.8 7.8 %shard_map.184.left_ref = bf16[1024,768]{1,0:T(8,128)(2,1)S(1)} custom-call(s32[2]{0:T(128)S(1)} %pad_add_fusion.1.ends_ref, bf16[1024,256]{1,0:T(8,128)(2,1)S(1)} %copy-done.28, bf16[1024,256]{1,0:T(8,128)(2,1)S(1)} %copy-done.30, bf16[1024,256]{1,0:T(8,128)(2,1)S(1)} %copy-done.32, bf16[1024,256]{1,0:T(8,128)(2,1)S(1)} %convolution_convert_fusion.4.g_ref, ...), custom_call_target="tpu_custom_call" | custom-call | tf_op jit(solution)/shard_map/pallas_call | solution.py:743
  412.7 19.2 %collective-permute-done.36 = bf16[2,256,512]{2,1,0:T(8,128)(2,1)} collective-permute-done((bf16[2,256,512]{2,1,0:T(8,128)(2,1)S(1)}, bf16[2,256,512]{2,1,0:T(8,128)(2,1)}, u32[]{:S(2)}, u32[]{:S(2)}) %collective-permute-start.36) | collective-permute-done | bytes 524320 | tf_op jit(solution)/shard_map/ppermute | solution.py:426
  431.9 4.7 all-to-all-start.5
  442.7 4.6 collective-permute-start.39
  455.0 25.9 %collective-permute-done.39 = bf16[2,256,512]{2,1,0:T(8,128)(2,1)} collective-permute-done((bf16[2,256,512]{2,1,0:T(8,128)(2,1)S(1)}, bf16[2,256,512]{2,1,0:T(8,128)(2,1)}, u32[]{:S(2)}, u32[]{:S(2)}) %collective-permute-start.39) | collective-permute-done | bytes 524320 | tf_op jit(solution)/shard_map/ppermute | solution.py:426
  483.5 4.0 all-to-all-start.6
  491.4 3.2 shard_map.187
  494.6 8.9 %collective-permute-done.42 = bf16[1,2,64,2048]{3,2,1,0:T(8,128)(2,1)S(1)} collective-permute-done((bf16[1,2,64,2048]{3,2,1,0:T(8,128)(2,1)}, bf16[1,2,64,2048]{3,2,1,0:T(8,128)(2,1)S(1)}, u32[]{:S(2)}, u32[]{:S(2)}) %collective-permute-start.42) | collective-permute-done | bytes 524320 | tf_op jit(solution)/shard_map/ppermute | solution.py:426
  503.5 22.3 %collective-permute-done.41 = bf16[2,256,768]{2,1,0:T(8,128)(2,1)} collective-permute-done((bf16[2,256,768]{2,1,0:T(8,128)(2,1)S(1)}, bf16[2,256,768]{2,1,0:T(8,128)(2,1)}, u32[]{:S(2)}, u32[]{:S(2)}) %collective-permute-start.41) | collective-permute-done | bytes 786464 | tf_op jit(solution)/shard_map/ppermute | solution.py:426
  528.8 5.0 all-to-all-start.7
  536.7 5.4 collective-permute-start.43
  543.2 3.5 collective-permute-start.45
  550.4 6.8 %collective-permute-done.45 = bf16[64,2048]{1,0:T(8,128)(2,1)} collective-permute-done((bf16[64,2048]{1,0:T(8,128)(2,1)S(1)}, bf16[64,2048]{1,0:T(8,128)(2,1)}, u32[]{:S(2)}, u32[]{:S(2)}) %collective-permute-start.45) | collective-permute-done | bytes 262176 | tf_op jit(solution)/shard_map/ppermute | solution.py:1122
  (319 shorter events, 162.2 us)
Async XLA Ops:
  9.5 26.6 %all-to-all-start = ((bf16[8,80,768]{2,1,0:T(8,128)(2,1)}), bf16[8,80,768]{2,1,0:T(8,128)(2,1)S(1)}, u32[]{:S(2)}, u32[]{:S(2)}) async-start(bf16[8,80,768]{2,1,0:T(8,128)(2,1)} %shard_map.170), calls=%async_computation | async-start | bytes 1966080 | tf_op jit(solution)/shard_map/all_to_all | solution.py:437
  14.1 77.7 %all-gather.5.cloned.1.call-start = ((), (), s32[]{:S(2)}) async-start(), calls=%async_computation.8 | async-start | bytes 4718592 | tf_op jit(solution)/shard_map/all_gather | solution.py:465
  14.4 18.7 %collective-permute-start.4 = (s32[18]{0:T(128)S(1)}, s32[18]{0:T(128)S(1)}, u32[]{:S(2)}, u32[]{:S(2)}) collective-permute-start(s32[18]{0:T(128)S(1)} %pad_add_fusion), channel_id=1, source_target_pairs={{0,8},{1,9},{2,10},{3,11},{4,12},{5,13},{6,14},{7,15},{8,0},{9,1},... | collective-permute-start | bytes 224 | tf_op jit(solution)/shard_map/ppermute | solution.py:426
  14.7 31.1 %collective-permute-start.2 = (bf16[256,2048]{1,0:T(8,128)(2,1)S(1)}, bf16[256,2048]{1,0:T(8,128)(2,1)S(1)}, u32[]{:S(2)}, u32[]{:S(2)}) collective-permute-start(bf16[256,2048]{1,0:T(8,128)(2,1)S(1)} %copy-done.15), channel_id=1, source_target_pairs={{0,16},{1,17},{2,18},{3,19},{4,20},{5,21},{6,22},{7,23},{8,24},{9,... | collective-permute-start | bytes 3145736 | tf_op jit(solution)/shard_map/ppermute | solution.py:426
  15.0 30.9 %collective-permute-start = (bf16[128,2048]{1,0:T(8,128)(2,1)}, bf16[128,2048]{1,0:T(8,128)(2,1)}, u32[]{:S(2)}, u32[]{:S(2)}) collective-permute-start(bf16[128,2048]{1,0:T(8,128)(2,1)} %param.11), channel_id=1, source_target_pairs={{0,0},{1,1},{2,2},{3,3},{4,8},{5,9},{6,10},{7,11},{8,4},{9,5},{10,... | collective-permute-start | bytes 1572872 | tf_op jit(solution)/shard_map/ppermute | solution.py:457
  20.4 25.5 %collective-permute-start.1 = (bf16[128,2048]{1,0:T(8,128)(2,1)}, bf16[128,2048]{1,0:T(8,128)(2,1)}, u32[]{:S(2)}, u32[]{:S(2)}) collective-permute-start(bf16[128,2048]{1,0:T(8,128)(2,1)} %param.18), channel_id=1, source_target_pairs={{0,0},{1,1},{2,2},{3,3},{4,8},{5,9},{6,10},{7,11},{8,4},{9,5},{10,... | collective-permute-start | bytes 1572872 | tf_op jit(solution)/shard_map/ppermute | solution.py:457
  25.7 20.1 %collective-permute-start.3 = (bf16[64,2048]{1,0:T(8,128)(2,1)}, bf16[64,2048]{1,0:T(8,128)(2,1)S(1)}, u32[]{:S(2)}, u32[]{:S(2)}) collective-permute-start(bf16[64,2048]{1,0:T(8,128)(2,1)} %param.13), channel_id=1, source_target_pairs={{0,0},{1,16},{2,2},{3,18},{4,4},{5,20},{6,6},{7,22},{8,8},{9,24},{... | collective-permute-start | bytes 786440 | tf_op jit(solution)/shard_map/ppermute | solution.py:990
  45.9 40.4 %collective-permute-start.7 = (bf16[512,768]{1,0:T(8,128)(2,1)S(1)}, bf16[512,768]{1,0:T(8,128)(2,1)}, u32[]{:S(2)}, u32[]{:S(2)}) collective-permute-start(bf16[512,768]{1,0:T(8,128)(2,1)S(1)} %bitcast.181), channel_id=1, source_target_pairs={{0,16},{1,17},{2,18},{3,19},{4,20},{5,21},{6,22},{7,23},{8,24},{9,... | collective-permute-start | bytes 2359304 | tf_op jit(solution)/shard_map/ppermute | solution.py:426
  48.7 24.4 %collective-permute-start.5 = (bf16[256,768]{1,0:T(8,128)(2,1)}, bf16[256,768]{1,0:T(8,128)(2,1)S(1)}, u32[]{:S(2)}, u32[]{:S(2)}) collective-permute-start(bf16[256,768]{1,0:T(8,128)(2,1)} %bitcast.208), channel_id=1, source_target_pairs={{0,4},{1,5},{2,6},{3,7},{4,0},{5,1},{6,2},{7,3},{8,12},{9,13},{10,... | collective-permute-start | bytes 1179656 | tf_op jit(solution)/shard_map/ppermute | solution.py:426
  51.0 35.3 %collective-permute-start.6 = (bf16[256,768]{1,0:T(8,128)(2,1)}, bf16[256,768]{1,0:T(8,128)(2,1)}, u32[]{:S(2)}, u32[]{:S(2)}) collective-permute-start(bf16[256,768]{1,0:T(8,128)(2,1)} %bitcast.207), channel_id=1, source_target_pairs={{0,4},{1,5},{2,6},{3,7},{4,0},{5,1},{6,2},{7,3},{8,12},{9,13},{10,... | collective-permute-start | bytes 1179656 | tf_op jit(solution)/shard_map/ppermute | solution.py:426
  91.8 18.1 %collective-permute-start.12 = (bf16[64,2048]{1,0:T(8,128)(2,1)S(1)}, bf16[64,2048]{1,0:T(8,128)(2,1)}, u32[]{:S(2)}, u32[]{:S(2)}) collective-permute-start(bf16[64,2048]{1,0:T(8,128)(2,1)S(1)} %copy-done.63), channel_id=1, source_target_pairs={{0,4},{1,5},{2,6},{3,7},{4,0},{5,1},{6,2},{7,3},{8,12},{9,13},{10,... | collective-permute-start | bytes 786440 | tf_op jit(solution)/shard_map/ppermute | solution.py:426
  91.8 23.8 %collective-permute-start.10 = (bf16[256,768]{1,0:T(8,128)(2,1)S(1)}, bf16[256,768]{1,0:T(8,128)(2,1)S(1)}, u32[]{:S(2)}, u32[]{:S(2)}) collective-permute-start(bf16[256,768]{1,0:T(8,128)(2,1)S(1)} %collective-permute-done.5.rest_1_), channel_id=1, source_target_pairs={{0,16},{1,17},{2,18},{3,19},{4,20},{5,21},{6,22},{7,23},{8,24},{9,... | collective-permute-start | bytes 1179656 | tf_op jit(solution)/shard_map/ppermute | solution.py:426
  92.0 24.3 %collective-permute-start.11 = (bf16[256,768]{1,0:T(8,128)(2,1)}, bf16[256,768]{1,0:T(8,128)(2,1)S(1)}, u32[]{:S(2)}, u32[]{:S(2)}) collective-permute-start(bf16[256,768]{1,0:T(8,128)(2,1)} %collective-permute-done.6.rest_2_), channel_id=1, source_target_pairs={{0,16},{1,17},{2,18},{3,19},{4,20},{5,21},{6,22},{7,23},{8,24},{9,... | collective-permute-start | bytes 1179656 | tf_op jit(solution)/shard_map/ppermute | solution.py:426
  93.2 22.3 %collective-permute-start.13 = (bf16[64,2048]{1,0:T(8,128)(2,1)}, bf16[64,2048]{1,0:T(8,128)(2,1)}, u32[]{:S(2)}, u32[]{:S(2)}) collective-permute-start(bf16[64,2048]{1,0:T(8,128)(2,1)} %get-tuple-element.169), channel_id=1, source_target_pairs={{0,4},{1,5},{2,6},{3,7},{4,0},{5,1},{6,2},{7,3},{8,12},{9,13},{10,... | collective-permute-start | bytes 786440 | tf_op jit(solution)/shard_map/ppermute | solution.py:426
  117.0 35.1 %all-to-all-start.1 = ((bf16[8,64,1024]{2,1,0:T(8,128)(2,1)}), bf16[8,64,1024]{2,1,0:T(8,128)(2,1)S(1)}, u32[]{:S(2)}, u32[]{:S(2)}) async-start(bf16[8,64,1024]{2,1,0:T(8,128)(2,1)} %shard_map.171), calls=%async_computation.1 | async-start | bytes 2097152 | tf_op jit(solution)/shard_map/all_to_all | solution.py:437
  120.8 125.2 %all-gather.9.cloned.1.call-start = ((), (), s32[]{:S(2)}) async-start(), calls=%async_computation.10 | async-start | bytes 4718592 | tf_op jit(solution)/shard_map/all_gather | solution.py:465
  121.5 21.6 %collective-permute-start.14 = (bf16[2,64,2048]{2,1,0:T(8,128)(2,1)}, bf16[2,64,2048]{2,1,0:T(8,128)(2,1)}, u32[]{:S(2)}, u32[]{:S(2)}) collective-permute-start(bf16[2,64,2048]{2,1,0:T(8,128)(2,1)} %maximum_select_fusion.1), channel_id=1, source_target_pairs={{0,16},{1,17},{2,18},{3,19},{4,20},{5,21},{6,22},{7,23},{8,24},{9,... | collective-permute-start | bytes 1572872 | tf_op jit(solution)/shard_map/ppermute | solution.py:426
  122.7 30.5 %collective-permute-start.15 = (bf16[64,2048]{1,0:T(8,128)(2,1)}, bf16[64,2048]{1,0:T(8,128)(2,1)}, u32[]{:S(2)}, u32[]{:S(2)}) collective-permute-start(bf16[64,2048]{1,0:T(8,128)(2,1)} %get-tuple-element.181), channel_id=1, source_target_pairs={{0,4},{1,5},{2,6},{3,7},{4,0},{5,1},{6,2},{7,3},{8,12},{9,13},{10,... | collective-permute-start | bytes 786440 | tf_op jit(solution)/shard_map/ppermute | solution.py:426
  124.7 29.1 %collective-permute-start.16 = (bf16[64,2048]{1,0:T(8,128)(2,1)}, bf16[64,2048]{1,0:T(8,128)(2,1)}, u32[]{:S(2)}, u32[]{:S(2)}) collective-permute-start(bf16[64,2048]{1,0:T(8,128)(2,1)} %get-tuple-element.182), channel_id=1, source_target_pairs={{0,4},{1,5},{2,6},{3,7},{4,0},{5,1},{6,2},{7,3},{8,12},{9,13},{10,... | collective-permute-start | bytes 786440 | tf_op jit(solution)/shard_map/ppermute | solution.py:426
  125.1 28.8 %collective-permute-start.17 = (bf16[64,2048]{1,0:T(8,128)(2,1)}, bf16[64,2048]{1,0:T(8,128)(2,1)}, u32[]{:S(2)}, u32[]{:S(2)}) collective-permute-start(bf16[64,2048]{1,0:T(8,128)(2,1)} %collective-permute-done.13.rest_2_), channel_id=1, source_target_pairs={{0,16},{1,17},{2,18},{3,19},{4,20},{5,21},{6,22},{7,23},{8,24},{9,... | collective-permute-start | bytes 786440 | tf_op jit(solution)/shard_map/ppermute | solution.py:426
  163.8 51.7 %all-to-all-start.2 = ((bf16[4,128,2048]{2,1,0:T(8,128)(2,1)}), bf16[4,128,2048]{2,1,0:T(8,128)(2,1)}, u32[]{:S(2)}, u32[]{:S(2)}) async-start(bf16[4,128,2048]{2,1,0:T(8,128)(2,1)} %bitcast.180), calls=%async_computation.2 | async-start | bytes 4194304 | tf_op jit(solution)/shard_map/all_to_all | solution.py:437
  173.8 87.5 %all-gather.7.cloned.1.call-start = ((), (), s32[]{:S(2)}) async-start(), calls=%async_computation.9 | async-start | bytes 4718592 | tf_op jit(solution)/shard_map/all_gather | solution.py:465
  174.2 40.4 %collective-permute-start.20 = (bf16[512,1024]{1,0:T(8,128)(2,1)S(1)}, bf16[512,1024]{1,0:T(8,128)(2,1)S(1)}, u32[]{:S(2)}, u32[]{:S(2)}) collective-permute-start(bf16[512,1024]{1,0:T(8,128)(2,1)S(1)} %bitcast.174), channel_id=1, source_target_pairs={{0,16},{1,17},{2,18},{3,19},{4,20},{5,21},{6,22},{7,23},{8,24},{9,... | collective-permute-start | bytes 3145736 | tf_op jit(solution)/shard_map/ppermute | solution.py:426
  175.0 39.6 %collective-permute-start.19 = (bf16[256,1024]{1,0:T(8,128)(2,1)}, bf16[256,1024]{1,0:T(8,128)(2,1)}, u32[]{:S(2)}, u32[]{:S(2)}) collective-permute-start(bf16[256,1024]{1,0:T(8,128)(2,1)} %bitcast.206), channel_id=1, source_target_pairs={{0,4},{1,5},{2,6},{3,7},{4,0},{5,1},{6,2},{7,3},{8,12},{9,13},{10,... | collective-permute-start | bytes 1572872 | tf_op jit(solution)/shard_map/ppermute | solution.py:426
  175.0 38.2 %collective-permute-start.21 = (bf16[64,2048]{1,0:T(8,128)(2,1)}, bf16[64,2048]{1,0:T(8,128)(2,1)S(1)}, u32[]{:S(2)}, u32[]{:S(2)}) collective-permute-start(bf16[64,2048]{1,0:T(8,128)(2,1)} %get-tuple-element.204), channel_id=1, source_target_pairs={{0,4},{1,5},{2,6},{3,7},{4,0},{5,1},{6,2},{7,3},{8,12},{9,13},{10,... | collective-permute-start | bytes 786440 | tf_op jit(solution)/shard_map/ppermute | solution.py:426
  177.3 35.9 %collective-permute-start.22 = (bf16[64,2048]{1,0:T(8,128)(2,1)}, bf16[64,2048]{1,0:T(8,128)(2,1)S(1)}, u32[]{:S(2)}, u32[]{:S(2)}) collective-permute-start(bf16[64,2048]{1,0:T(8,128)(2,1)} %collective-permute-done.15.rest_3_), channel_id=1, source_target_pairs={{0,16},{1,17},{2,18},{3,19},{4,20},{5,21},{6,22},{7,23},{8,24},{9,... | collective-permute-start | bytes 786440 | tf_op jit(solution)/shard_map/ppermute | solution.py:426
  178.1 35.8 %collective-permute-start.23 = (bf16[64,2048]{1,0:T(8,128)(2,1)}, bf16[64,2048]{1,0:T(8,128)(2,1)S(1)}, u32[]{:S(2)}, u32[]{:S(2)}) collective-permute-start(bf16[64,2048]{1,0:T(8,128)(2,1)} %collective-permute-done.16.rest_4_), channel_id=1, source_target_pairs={{0,16},{1,17},{2,18},{3,19},{4,20},{5,21},{6,22},{7,23},{8,24},{9,... | collective-permute-start | bytes 786440 | tf_op jit(solution)/shard_map/ppermute | solution.py:426
  219.0 26.5 %collective-permute-start.24 = (bf16[256,1024]{1,0:T(8,128)(2,1)}, bf16[256,1024]{1,0:T(8,128)(2,1)}, u32[]{:S(2)}, u32[]{:S(2)}) collective-permute-start(bf16[256,1024]{1,0:T(8,128)(2,1)} %bitcast.205), channel_id=1, source_target_pairs={{0,4},{1,5},{2,6},{3,7},{4,0},{5,1},{6,2},{7,3},{8,12},{9,13},{10,... | collective-permute-start | bytes 1572872 | tf_op jit(solution)/shard_map/ppermute | solution.py:426
  222.8 33.3 %collective-permute-start.25 = (bf16[256,1024]{1,0:T(8,128)(2,1)}, bf16[256,1024]{1,0:T(8,128)(2,1)}, u32[]{:S(2)}, u32[]{:S(2)}) collective-permute-start(bf16[256,1024]{1,0:T(8,128)(2,1)} %collective-permute-done.19.rest_1_), channel_id=1, source_target_pairs={{0,16},{1,17},{2,18},{3,19},{4,20},{5,21},{6,22},{7,23},{8,24},{9,... | collective-permute-start | bytes 1572872 | tf_op jit(solution)/shard_map/ppermute | solution.py:426
  288.2 45.7 %all-to-all-start.3 = ((bf16[4,128,2048]{2,1,0:T(8,128)(2,1)}), bf16[4,128,2048]{2,1,0:T(8,128)(2,1)}, u32[]{:S(2)}, u32[]{:S(2)}) async-start(bf16[4,128,2048]{2,1,0:T(8,128)(2,1)} %bitcast.48), calls=%async_computation.3 | async-start | bytes 4194304 | tf_op jit(solution)/shard_map/all_to_all | solution.py:437
  292.8 91.6 %all-gather.11.cloned.1.call-start = ((), (), s32[]{:S(2)}) async-start(), calls=%async_computation.11 | async-start | bytes 4718592 | tf_op jit(solution)/shard_map/all_gather | solution.py:465
  297.9 36.0 %collective-permute-start.29 = (bf16[1,2,256,1536]{3,2,1,0:T(8,128)(2,1)}, bf16[1,2,256,1536]{3,2,1,0:T(8,128)(2,1)}, u32[]{:S(2)}, u32[]{:S(2)}) collective-permute-start(bf16[1,2,256,1536]{3,2,1,0:T(8,128)(2,1)} %bitcast.47), channel_id=1, source_target_pairs={{0,16},{1,17},{2,18},{3,19},{4,20},{5,21},{6,22},{7,23},{8,24},{9,... | collective-permute-start | bytes 4718600 | tf_op jit(solution)/shard_map/ppermute | solution.py:426
  300.9 25.9 %collective-permute-start.30 = (bf16[1,2,256,512]{3,2,1,0:T(8,128)(2,1)S(1)}, bf16[1,2,256,512]{3,2,1,0:T(8,128)(2,1)}, u32[]{:S(2)}, u32[]{:S(2)}) collective-permute-start(bf16[1,2,256,512]{3,2,1,0:T(8,128)(2,1)S(1)} %dynamic-slice_bitcast_fusion.1), channel_id=1, source_target_pairs={{0,4},{1,5},{2,6},{3,7},{4,0},{5,1},{6,2},{7,3},{8,12},{9,13},{10,... | collective-permute-start | bytes 1572872 | tf_op jit(solution)/shard_map/ppermute | solution.py:426
  344.1 15.6 %collective-permute-start.34 = (bf16[512,2048]{1,0:T(8,128)(2,1)}, bf16[512,2048]{1,0:T(8,128)(2,1)}, u32[]{:S(2)}, u32[]{:S(2)}) collective-permute-start(bf16[512,2048]{1,0:T(8,128)(2,1)} %shard_map.182), channel_id=1, source_target_pairs={{0,8},{1,9},{2,10},{3,11},{4,12},{5,13},{6,14},{7,15},{8,0},{9,1},... | collective-permute-start | bytes 6291464 | tf_op jit(solution)/shard_map/ppermute | solution.py:426
  347.1 36.4 %collective-permute-start.33 = (bf16[1,256,1536]{2,1,0:T(8,128)(2,1)S(1)}, bf16[1,256,1536]{2,1,0:T(8,128)(2,1)S(1)}, u32[]{:S(2)}, u32[]{:S(2)}) collective-permute-start(bf16[1,256,1536]{2,1,0:T(8,128)(2,1)S(1)} %fusion.25), channel_id=1, source_target_pairs={{0,4},{1,5},{2,6},{3,7},{4,0},{5,1},{6,2},{7,3},{8,12},{9,13},{10,... | collective-permute-start | bytes 2359304 | tf_op jit(solution)/shard_map/ppermute | solution.py:426
  348.5 35.9 %collective-permute-start.31 = (bf16[2,2,256,512]{3,2,0,1:T(8,128)(2,1)S(1)}, bf16[2,2,256,512]{3,2,0,1:T(8,128)(2,1)}, u32[]{:S(2)}, u32[]{:S(2)}) collective-permute-start(bf16[2,2,256,512]{3,2,0,1:T(8,128)(2,1)S(1)} %copy.68), channel_id=1, source_target_pairs={{0,16},{1,17},{2,18},{3,19},{4,20},{5,21},{6,22},{7,23},{8,24},{9,... | collective-permute-start | bytes 3145736 | tf_op jit(solution)/shard_map/ppermute | solution.py:426
  349.9 29.1 %collective-permute-start.32 = (bf16[1,256,512]{2,1,0:T(8,128)(2,1)S(1)}, bf16[1,256,512]{2,1,0:T(8,128)(2,1)S(1)}, u32[]{:S(2)}, u32[]{:S(2)}) collective-permute-start(bf16[1,256,512]{2,1,0:T(8,128)(2,1)S(1)} %fusion.56), channel_id=1, source_target_pairs={{0,16},{1,17},{2,18},{3,19},{4,20},{5,21},{6,22},{7,23},{8,24},{9,... | collective-permute-start | bytes 786440 | tf_op jit(solution)/shard_map/ppermute | solution.py:426
  384.4 47.5 %all-to-all-start.4 = ((bf16[4,128,2048]{2,1,0:T(8,128)(2,1)}), bf16[4,128,2048]{2,1,0:T(8,128)(2,1)}, u32[]{:S(2)}, u32[]{:S(2)}) async-start(bf16[4,128,2048]{2,1,0:T(8,128)(2,1)} %bitcast.61), calls=%async_computation.4 | async-start | bytes 4194304 | tf_op jit(solution)/shard_map/all_to_all | solution.py:437
  404.9 27.1 %collective-permute-start.35 = (bf16[2,2,256,512]{3,2,0,1:T(8,128)(2,1)S(1)}, bf16[2,2,256,512]{3,2,0,1:T(8,128)(2,1)}, u32[]{:S(2)}, u32[]{:S(2)}) collective-permute-start(bf16[2,2,256,512]{3,2,0,1:T(8,128)(2,1)S(1)} %copy.69), channel_id=1, source_target_pairs={{0,16},{1,17},{2,18},{3,19},{4,20},{5,21},{6,22},{7,23},{8,24},{9,... | collective-permute-start | bytes 3145736 | tf_op jit(solution)/shard_map/ppermute | solution.py:426
  406.6 25.3 %collective-permute-start.36 = (bf16[2,256,512]{2,1,0:T(8,128)(2,1)S(1)}, bf16[2,256,512]{2,1,0:T(8,128)(2,1)}, u32[]{:S(2)}, u32[]{:S(2)}) collective-permute-start(bf16[2,256,512]{2,1,0:T(8,128)(2,1)S(1)} %fusion.43), channel_id=1, source_target_pairs={{0,4},{1,5},{2,6},{3,7},{4,0},{5,1},{6,2},{7,3},{8,12},{9,13},{10,... | collective-permute-start | bytes 1572872 | tf_op jit(solution)/shard_map/ppermute | solution.py:426
  431.9 48.9 %all-to-all-start.5 = ((bf16[4,128,2048]{2,1,0:T(8,128)(2,1)}), bf16[4,128,2048]{2,1,0:T(8,128)(2,1)}, u32[]{:S(2)}, u32[]{:S(2)}) async-start(bf16[4,128,2048]{2,1,0:T(8,128)(2,1)} %bitcast.179), calls=%async_computation.5 | async-start | bytes 4194304 | tf_op jit(solution)/shard_map/all_to_all | solution.py:437
  436.8 44.1 %collective-permute-start.38 = (bf16[2,2,256,768]{3,2,0,1:T(8,128)(2,1)S(1)}, bf16[2,2,256,768]{3,2,0,1:T(8,128)(2,1)}, u32[]{:S(2)}, u32[]{:S(2)}) collective-permute-start(bf16[2,2,256,768]{3,2,0,1:T(8,128)(2,1)S(1)} %copy.71), channel_id=1, source_target_pairs={{0,16},{1,17},{2,18},{3,19},{4,20},{5,21},{6,22},{7,23},{8,24},{9,... | collective-permute-start | bytes 4718600 | tf_op jit(solution)/shard_map/ppermute | solution.py:426
  442.7 38.2 %collective-permute-start.39 = (bf16[2,256,512]{2,1,0:T(8,128)(2,1)S(1)}, bf16[2,256,512]{2,1,0:T(8,128)(2,1)}, u32[]{:S(2)}, u32[]{:S(2)}) collective-permute-start(bf16[2,256,512]{2,1,0:T(8,128)(2,1)S(1)} %fusion.42), channel_id=1, source_target_pairs={{0,4},{1,5},{2,6},{3,7},{4,0},{5,1},{6,2},{7,3},{8,12},{9,13},{10,... | collective-permute-start | bytes 1572872 | tf_op jit(solution)/shard_map/ppermute | solution.py:426
  483.5 42.3 %all-to-all-start.6 = ((bf16[8,64,1024]{2,1,0:T(8,128)(2,1)}), bf16[8,64,1024]{2,1,0:T(8,128)(2,1)S(1)}, u32[]{:S(2)}, u32[]{:S(2)}) async-start(bf16[8,64,1024]{2,1,0:T(8,128)(2,1)} %pad_maximum_fusion.1), calls=%async_computation.6 | async-start | bytes 2097152 | tf_op jit(solution)/shard_map/all_to_all | solution.py:437
  489.1 36.7 %collective-permute-start.41 = (bf16[2,256,768]{2,1,0:T(8,128)(2,1)S(1)}, bf16[2,256,768]{2,1,0:T(8,128)(2,1)}, u32[]{:S(2)}, u32[]{:S(2)}) collective-permute-start(bf16[2,256,768]{2,1,0:T(8,128)(2,1)S(1)} %fusion.24), channel_id=1, source_target_pairs={{0,4},{1,5},{2,6},{3,7},{4,0},{5,1},{6,2},{7,3},{8,12},{9,13},{10,... | collective-permute-start | bytes 2359304 | tf_op jit(solution)/shard_map/ppermute | solution.py:426
  525.9 16.2 %collective-permute-start.44 = (bf16[1,64,2048]{2,1,0:T(8,128)(2,1)S(1)}, bf16[1,64,2048]{2,1,0:T(8,128)(2,1)S(1)}, u32[]{:S(2)}, u32[]{:S(2)}) collective-permute-start(bf16[1,64,2048]{2,1,0:T(8,128)(2,1)S(1)} %fusion.53), channel_id=1, source_target_pairs={{0,4},{1,5},{2,6},{3,7},{4,0},{5,1},{6,2},{7,3},{8,12},{9,13},{10,... | collective-permute-start | bytes 786440 | tf_op jit(solution)/shard_map/ppermute | solution.py:426
  528.8 30.1 %all-to-all-start.7 = ((bf16[8,64,768]{2,1,0:T(8,128)(2,1)}), bf16[8,64,768]{2,1,0:T(8,128)(2,1)S(1)}, u32[]{:S(2)}, u32[]{:S(2)}) async-start(bf16[8,64,768]{2,1,0:T(8,128)(2,1)} %bitcast.83), calls=%async_computation.7 | async-start | bytes 1572864 | tf_op jit(solution)/shard_map/all_to_all | solution.py:437
  536.7 22.2 %collective-permute-start.43 = (bf16[128,2048]{1,0:T(8,128)(2,1)}, bf16[128,2048]{1,0:T(8,128)(2,1)}, u32[]{:S(2)}, u32[]{:S(2)}) collective-permute-start(bf16[128,2048]{1,0:T(8,128)(2,1)} %shard_map.187), channel_id=1, source_target_pairs={{0,0},{1,1},{2,2},{3,3},{4,8},{5,9},{6,10},{7,11},{8,4},{9,5},{10,... | collective-permute-start | bytes 1572872 | tf_op jit(solution)/shard_map/ppermute | solution.py:457
  (82 other events, 716.8 us)
Sparse Core Ops, SparseCore 0:
  46.0 45.6 all-gather.4
  123.2 40.1 all-gather.8
  219.2 42.0 all-gather.6
  338.1 45.1 all-gather.10
